TPU v7x, 256 devices: a whole 4x4x8 slice. The times are simulated.
256 devices in a mesh: seq: 32 (over y_hi, z, core), head: 8 (over y_lo, x).
Axes of the slice: x: 4, y: 4 (y_hi: 2, y_lo: 2; y = y_hi * 2 + y_lo), z: 8, core: 2. Of those that a mesh axis runs over, the one named last changes fastest.
Arguments:
- query_proj: bfloat16 [12288, 2048], P('seq', 'head'), may hold values from -100 to 100
- key_proj: bfloat16 [12288, 2048], P('seq', 'head'), may hold values from -4 to 4
- value_proj: bfloat16 [12288, 2048], P('seq', 'head'), may hold values from -6 to 6
- query_tangent: bfloat16 [12288, 2048], P('seq', 'head'), may hold values from -6 to 6
- key_tangent: bfloat16 [12288, 2048], P('seq', 'head'), may hold values from -6 to 6
- value_tangent: bfloat16 [12288, 2048], P('seq', 'head'), may hold values from -16 to 16
Outputs:
- attended: bfloat16 [12288, 2048], P('seq', 'head')
- tangent_unit: bfloat16 [12288, 2048], P('seq', 'head')
All inputs are finite; a program needn't handle non-finite values.
Results may differ from a plain program's by a relative error of at most 0.0095.
Values may be sent and summed in bfloat16 or wider, within the bound.
No kernel may reach another device: no remote copies, remote signals or barrier semaphores. Data moves between devices by JAX's collectives and lax.ppermute only.
A program may use at most 128 MiB of HBM per device.

v0:
```python
import math

import jax
import jax.numpy as jnp
from jax import lax
from jax.sharding import PartitionSpec as P

HEADS = 16
DH = 128


def on_device(query_proj, key_proj, value_proj, query_tangent, key_tangent, value_tangent):
    tok_rows = query_proj.shape[0]
    width = query_proj.shape[1]
    head_count = width // DH
    scale_factor = 1.0 / math.sqrt(DH)
    query_heads = query_proj.reshape(tok_rows, head_count, DH)
    query_theads = query_tangent.reshape(tok_rows, head_count, DH)

    def split_blocks(piece):
        length = piece.shape[0]
        block = math.gcd(length, 1536)
        return piece.reshape(length // block, block, head_count, DH)

    def scores_of(key_block):
        return (
            jnp.einsum("thd,nhd->htn", query_heads, key_block, preferred_element_type=jnp.float32)
            * scale_factor
        )

    def tangent_of(key_block, key_tblock):
        first = jnp.einsum(
            "thd,nhd->htn", query_theads, key_block, preferred_element_type=jnp.float32
        )
        second = jnp.einsum(
            "thd,nhd->htn", query_heads, key_tblock, preferred_element_type=jnp.float32
        )
        return (first + second) * scale_factor

    def apply_values(weight_bf, value_block):
        return jnp.einsum(
            "htn,nhd->htd", weight_bf, value_block, preferred_element_type=jnp.float32
        )

    row_zeros = jnp.zeros((head_count, tok_rows), jnp.float32)
    acc_zeros = jnp.zeros((head_count, tok_rows, DH), jnp.float32)
    lowest = jnp.full((head_count, tok_rows), -jnp.inf, jnp.float32)
    state = (lowest, row_zeros, row_zeros, acc_zeros, acc_zeros, acc_zeros)
    pieces = (
        lax.all_gather(key_proj, "seq", axis=0, tiled=True),
        lax.all_gather(value_proj, "seq", axis=0, tiled=True),
        lax.all_gather(key_tangent, "seq", axis=0, tiled=True),
        lax.all_gather(value_tangent, "seq", axis=0, tiled=True),
    )

    def inner(inner_state, blocks):
        key_block, value_block, key_tblock, value_tblock = blocks
        running_max, total, cross, primal_acc, shift_acc, direct_acc = inner_state
        scores = scores_of(key_block)
        score_tan = tangent_of(key_block, key_tblock)
        new_max = jnp.maximum(running_max, jnp.max(scores, axis=2))
        factor = jnp.exp(running_max - new_max)
        weights = jnp.exp(scores - new_max[..., None])
        tilted = weights * score_tan
        total = total * factor + jnp.sum(weights, axis=2)
        cross = cross * factor + jnp.sum(tilted, axis=2)
        weight_bf = weights.astype(jnp.bfloat16)
        tilted_bf = tilted.astype(jnp.bfloat16)
        primal_acc = primal_acc * factor[..., None] + apply_values(weight_bf, value_block)
        shift_acc = shift_acc * factor[..., None] + apply_values(tilted_bf, value_block)
        direct_acc = direct_acc * factor[..., None] + apply_values(weight_bf, value_tblock)
        return ((new_max, total, cross, primal_acc, shift_acc, direct_acc), None)

    stacked = tuple((split_blocks(piece) for piece in pieces))
    state, unused = lax.scan(inner, state, stacked)
    running_max, total, cross, primal_acc, shift_acc, direct_acc = state
    primal_out = primal_acc / total[..., None]
    tangent_out = (shift_acc + direct_acc) / total[..., None] - (cross / total)[
        ..., None
    ] * primal_out
    primal_rows = primal_out.transpose(1, 0, 2).reshape(tok_rows, width)
    tangent_rows = tangent_out.transpose(1, 0, 2).reshape(tok_rows, width)
    local_squares = jnp.sum(tangent_rows * tangent_rows, axis=1)
    all_squares = lax.psum(local_squares, "head")
    rms = jnp.sqrt(all_squares / (HEADS * DH) + 1e-06)
    return (primal_rows.astype(jnp.bfloat16), (tangent_rows / rms[:, None]).astype(jnp.bfloat16))


def solution(mesh):
    return jax.shard_map(
        on_device,
        mesh=mesh,
        in_specs=(
            P("seq", "head"),
            P("seq", "head"),
            P("seq", "head"),
            P("seq", "head"),
            P("seq", "head"),
            P("seq", "head"),
        ),
        out_specs=(P("seq", "head"), P("seq", "head")),
        check_vma=False,
    )
```

profile of v0, /device:TPU:1, one launch (start us, length us, event | category | flops | bytes accessed | tf_op | source)
XLA Modules:
  0.0 552.8 jit_solution(11158130588044027408)
XLA Ops:
  12.6 97.0 %all-gather.5.cloned.1.call-done = bf16[12288,256]{1,0:T(8,128)(2,1)} async-done(((bf16[384,256]{1,0:T(8,128)(2,1)}), bf16[12288,256]{1,0:T(8,128)(2,1)}) %all-gather.5.cloned.1.call-update) | async-done | bytes 6291472 | tf_op jit(solution)/shard_map/all_gather | solution.py:50
  109.5 9.7 %reshape.39 = bf16[8,1536,2,128]{3,2,1,0:T(2,128)(2,1)} reshape(bf16[12288,256]{1,0:T(8,128)(2,1)} %all-gather.5.cloned.1.call-done) | data formatting | bytes 12582912 | tf_op jit(solution)/shard_map/reshape | solution.py:23
  119.2 84.2 %all-gather.7.cloned.1.call-done = bf16[12288,256]{1,0:T(8,128)(2,1)} async-done(((bf16[384,256]{1,0:T(8,128)(2,1)}), bf16[12288,256]{1,0:T(8,128)(2,1)}) %all-gather.7.cloned.1.call-update) | async-done | bytes 6291472 | tf_op jit(solution)/shard_map/all_gather | solution.py:52
  203.4 9.7 %reshape.40 = bf16[8,1536,2,128]{3,2,1,0:T(2,128)(2,1)} reshape(bf16[12288,256]{1,0:T(8,128)(2,1)} %all-gather.7.cloned.1.call-done) | data formatting | bytes 12582912 | tf_op jit(solution)/shard_map/reshape | solution.py:23
  213.1 84.2 %all-gather.9.cloned.1.call-done = bf16[12288,256]{1,0:T(8,128)(2,1)} async-done(((bf16[384,256]{1,0:T(8,128)(2,1)}), bf16[12288,256]{1,0:T(8,128)(2,1)}) %all-gather.9.cloned.1.call-update) | async-done | bytes 6291472 | tf_op jit(solution)/shard_map/all_gather | solution.py:51
  297.3 9.8 %reshape.41 = bf16[8,1536,2,128]{3,2,1,0:T(2,128)(2,1)} reshape(bf16[12288,256]{1,0:T(8,128)(2,1)} %all-gather.9.cloned.1.call-done) | data formatting | bytes 12582912 | tf_op jit(solution)/shard_map/reshape | solution.py:23
  307.1 84.0 %all-gather.11.cloned.1.call-done = bf16[12288,256]{1,0:T(8,128)(2,1)} async-done(((bf16[384,256]{1,0:T(8,128)(2,1)}), bf16[12288,256]{1,0:T(8,128)(2,1)}) %all-gather.11.cloned.1.call-update) | async-done | bytes 6291472 | tf_op jit(solution)/shard_map/all_gather | solution.py:53
  391.1 9.7 %reshape.42 = bf16[8,1536,2,128]{3,2,1,0:T(2,128)(2,1)} reshape(bf16[12288,256]{1,0:T(8,128)(2,1)} %all-gather.11.cloned.1.call-done) | data formatting | bytes 12582912 | tf_op jit(solution)/shard_map/reshape | solution.py:23
  400.8 128.6 %while.21 = (s32[]{:T(128)}, f32[2,384]{1,0:T(2,128)S(1)}, f32[2,384]{1,0:T(2,128)S(1)}, f32[2,384]{1,0:T(2,128)S(1)}, f32[2,384,128]{2,1,0:T(8,128)S(1)}, /*ind...) while((s32[]{:T(128)}, f32[2,384]{1,0:T(2,128)S(1)}, ...), condition=%wide.region_4.5_spmd.clone, body=%wide.region_0.4_spmd.clone.sunk | while | flops 1834063104 | bytes 70659264 | solution.py:75
  400.8 2.2 constant_dynamic-slice_fusion.6
  403.0 2.9 bitcast_reduce_fusion.2
  406.7 1.5 copy-done
  408.2 1.7 fusion.47
  409.9 2.2 constant_dynamic-slice_fusion.7
  412.2 1.4 convolution_add_fusion.5
  414.6 1.4 convolution_add_fusion.4
  416.8 2.2 constant_dynamic-slice_fusion.6
  419.1 2.9 bitcast_reduce_fusion.2
  422.7 1.5 copy-done
  424.3 1.7 fusion.47
  426.0 2.2 constant_dynamic-slice_fusion.7
  428.2 1.4 convolution_add_fusion.5
  430.7 1.4 convolution_add_fusion.4
  432.9 2.2 constant_dynamic-slice_fusion.6
  435.2 2.9 bitcast_reduce_fusion.2
  438.8 1.5 copy-done
  440.4 1.7 fusion.47
  442.1 2.2 constant_dynamic-slice_fusion.7
  444.3 1.4 convolution_add_fusion.5
  446.8 1.4 convolution_add_fusion.4
  449.0 2.2 constant_dynamic-slice_fusion.6
  451.2 2.9 bitcast_reduce_fusion.2
  454.9 1.5 copy-done
  456.4 1.7 fusion.47
  458.1 2.2 constant_dynamic-slice_fusion.7
  460.4 1.4 convolution_add_fusion.5
  462.8 1.4 convolution_add_fusion.4
  465.1 2.2 constant_dynamic-slice_fusion.6
  467.3 2.9 bitcast_reduce_fusion.2
  471.0 1.5 copy-done
  472.5 1.7 fusion.47
  474.2 2.2 constant_dynamic-slice_fusion.7
  476.5 1.4 convolution_add_fusion.5
  478.9 1.4 convolution_add_fusion.4
  481.1 2.2 constant_dynamic-slice_fusion.6
  483.4 2.9 bitcast_reduce_fusion.2
  487.0 1.5 copy-done
  488.6 1.7 fusion.47
  490.3 2.2 constant_dynamic-slice_fusion.7
  492.5 1.4 convolution_add_fusion.5
  495.0 1.4 convolution_add_fusion.4
  497.2 2.2 constant_dynamic-slice_fusion.6
  499.5 2.9 bitcast_reduce_fusion.2
  503.1 1.5 copy-done
  504.7 1.7 fusion.47
  506.4 2.2 constant_dynamic-slice_fusion.7
  513.3 2.2 constant_dynamic-slice_fusion.6
  515.5 2.9 bitcast_reduce_fusion.2
  519.2 1.5 copy-done
  520.7 1.7 fusion.47
  522.4 2.2 constant_dynamic-slice_fusion.7
  524.7 1.4 convolution_add_fusion.5
  527.1 1.4 convolution_add_fusion.4
  530.6 14.9 %psum.7 = f32[384]{0:T(512)S(1)} all-reduce(f32[384]{0:T(512)S(1)} %get-tuple-element.161), channel_id=1, replica_groups=mesh['seq'=32,'head'=8] {'head'}, use_global_device_ids=true, to_apply=%region_6.7 | all-reduce | flops 384 | bytes 3072 | tf_op jit(solution)/shard_map/psum | solution.py:84
  (89 shorter events, 31.3 us)
Async XLA Ops:
  7.2 102.4 %all-gather.5.cloned.1.call-start = ((), (), s32[]{:S(2)}) async-start(), calls=%async_computation | async-start | bytes 6488064 | tf_op jit(solution)/shard_map/all_gather | solution.py:50
  7.9 195.5 %all-gather.7.cloned.1.call-start = ((), (), s32[]{:S(2)}) async-start(), calls=%async_computation.1 | async-start | bytes 6488064 | tf_op jit(solution)/shard_map/all_gather | solution.py:52
  8.6 288.7 %all-gather.9.cloned.1.call-start = ((), (), s32[]{:S(2)}) async-start(), calls=%async_computation.2 | async-start | bytes 6488064 | tf_op jit(solution)/shard_map/all_gather | solution.py:51
  9.4 381.7 %all-gather.11.cloned.1.call-start = ((), (), s32[]{:S(2)}) async-start(), calls=%async_computation.3 | async-start | bytes 6488064 | tf_op jit(solution)/shard_map/all_gather | solution.py:53
  405.9 2.3 copy-start
  421.9 2.3 copy-start
  438.0 2.3 copy-start
  454.1 2.3 copy-start
  470.2 2.3 copy-start
  486.2 2.3 copy-start
  502.3 2.3 copy-start
  518.4 2.3 copy-start
Sparse Core Ops, SparseCore 0:
  10.8 98.7 all-gather.4
  112.3 91.0 all-gather.6
  206.2 91.0 all-gather.8
  299.9 91.0 all-gather.10
where the time goes:
time: 557 us; the launch traced here: 553 us
  waiting for transfers between devices  352 us (63%)
  local copies, waits for them, and re-layouts  89.7 us (16%)
  matrix products  73.2 us (13%)
  blocking collectives  14.9 us (3%)
  between operations  13.8 us (2%)
  other arithmetic  8.63 us (2%)
    all_gather x1, waiting for transfers between devices, on_device(): lax.all_gather(key_proj, 'seq', axis=0, tiled=True)  97 us
    all_gather x1, waiting for transfers between devices, on_device(): lax.all_gather(key_tangent, 'seq', axis=0, tiled=True)  84.2 us
    all_gather x1, waiting for transfers between devices, on_device(): lax.all_gather(value_proj, 'seq', axis=0, tiled=True)  84.2 us
    all_gather x1, waiting for transfers between devices, on_device(): lax.all_gather(value_tangent, 'seq', axis=0, tiled=True)  84 us
    reshape x4, local copies, waits for them, and re-layouts, split_blocks(): return piece.reshape(length // block, block, head_count, DH)  38.9 us
    dynamic_slice x16, local copies, waits for them, and re-layouts, on_device(): state, unused = lax.scan(inner, state, stacked)  35.9 us
    dot_general x24, matrix products, apply_values(): jnp.einsum('htn,nhd->htd', weight_bf, value_block, preferred_element_type...  30.6 us
    dot_general x8, matrix products, scores_of(): jnp.einsum('thd,nhd->htn', query_heads, key_block, preferred_element_type...  22.9 us
  transfers between devices with their start and end apart: 4, of which 4 were waited for; matrix products, arithmetic and copies ran while one was open for 6% of the time, Pallas kernels for 0%

commit v1 on v0

v1 whole, which is shorter than its diff:
```python
import functools
import math

import jax
import jax.numpy as jnp
from jax import lax
from jax.experimental import pallas as pl
from jax.experimental.pallas import tpu as pltpu
from jax.sharding import Mesh
from jax.sharding import PartitionSpec as P

HEADS = 16
DH = 128
SCALE = 1.0 / math.sqrt(DH)
LOG2E = math.log2(math.e)
F32 = jnp.float32
BF16 = jnp.bfloat16
MIB = 1 << 20
SWAP = ((0, 1), (1, 0))


def params(limit):
    return pltpu.CompilerParams(vmem_limit_bytes=limit * MIB)


def pack_kernel(q, k, v, qt, kt, vt, own_kv, own_q, other_kv, other_q):
    flip = lax.axis_index("yh") == 1
    spots = ((kt, 0, 0), (k, 0, 1), (v, 0, 2), (vt, 0, 3), (q, 1, 0), (qt, 1, 1))
    for ref, which, at in spots:
        low, high = ref[:, :DH], ref[:, DH:]
        cols = slice(at * DH, (at + 1) * DH)
        (own_kv, own_q)[which][:, cols] = jnp.where(flip, high, low)
        (other_kv, other_q)[which][:, cols] = jnp.where(flip, low, high)


def pack(*arrays):
    rows = arrays[0].shape[0]
    kv = jax.ShapeDtypeStruct((rows, 4 * DH), BF16)
    qq = jax.ShapeDtypeStruct((rows, 2 * DH), BF16)
    return pl.pallas_call(
        pack_kernel,
        out_shape=(kv, qq, kv, qq),
        compiler_params=params(16),
        cost_estimate=pl.CostEstimate(flops=0, bytes_accessed=12 * rows * 2 * DH * 2, transcendentals=0),
        name="pack",
    )(*arrays)


def nt(a, b):
    return lax.dot_general(a, b, (((1,), (1,)), ((), ())), preferred_element_type=F32)


def nn(a, b):
    return lax.dot_general(a, b, (((1,), (0,)), ((), ())), preferred_element_type=F32)


def attend_kernel(blocks, first, last, tiles, *refs):
    q_ref = refs[0]
    kv_refs = refs[1 : 1 + blocks]
    at = 1 + blocks
    if not first:
        acc_ref, stat_ref = refs[at : at + 2]
        at += 2
    outs = refs[at:-1]
    kv = refs[-1]
    rows = kv_refs[0].shape[0]
    step = pl.program_id(0)

    @pl.when(step == 0)
    def _():
        for i, ref in enumerate(kv_refs):
            kv[i * rows : (i + 1) * rows, :] = ref[...]

    query = q_ref[...]
    scores = nt(query[:, :DH], kv[:, DH : 2 * DH]) * (SCALE * LOG2E)
    tangent = nt(query, kv[:, : 2 * DH])
    top = jnp.max(scores, axis=1, keepdims=True)
    if not first:
        old_top = stat_ref[:, 0:1]
        top = jnp.maximum(top, old_top)
    weights = jnp.exp2(scores - top)
    tilted = weights * tangent
    total = jnp.sum(weights, axis=1, keepdims=True)
    cross = jnp.sum(tilted, axis=1, keepdims=True)
    both = nn(weights.astype(BF16), kv[:, 2 * DH :])
    shift = nn(tilted.astype(BF16), kv[:, 2 * DH : 3 * DH]) * SCALE
    primal = both[:, :DH]
    moved = both[:, DH:] + shift
    if not first:
        factor = jnp.exp2(old_top - top)
        total = total + stat_ref[:, 1:2] * factor
        cross = cross + stat_ref[:, 2:3] * factor
        primal = primal + acc_ref[:, :DH] * factor
        moved = moved + acc_ref[:, DH:] * factor
    lane = lax.broadcasted_iota(jnp.int32, (query.shape[0], DH), 1)
    if last:
        near, near_stat, far, far_stat = outs
        inverse = 1.0 / total
        primal = primal * inverse
        moved = moved * inverse
        stat = jnp.where(lane == 0, top + jnp.log2(total), cross * (SCALE * inverse))

        @pl.when(step < tiles // 2)
        def _():
            near[:, :DH] = primal
            near[:, DH:] = moved
            near_stat[...] = stat

        @pl.when(step >= tiles // 2)
        def _():
            far[:, :DH] = primal.astype(BF16)
            far[:, DH:] = moved.astype(BF16)
            far_stat[...] = stat
    else:
        acc, stats = outs
        acc[:, :DH] = primal
        acc[:, DH:] = moved
        stats[...] = jnp.where(lane == 0, top, jnp.where(lane == 1, total, cross))


def attend(query, kvs, state, last=False, tile=256):
    rows = query.shape[0]
    tiles = rows // tile
    keys = sum(kv.shape[0] for kv in kvs)
    row_block = lambda width: pl.BlockSpec((tile, width), lambda i: (i, 0))
    whole = lambda a: pl.BlockSpec(a.shape, lambda i: (0, 0), pipeline_mode=pl.Buffered(1))
    ins = [query, *kvs]
    in_specs = [row_block(2 * DH)] + [whole(kv) for kv in kvs]
    if state is not None:
        ins += state
        in_specs += [row_block(2 * DH), row_block(DH)]
    if last:
        half = tiles // 2
        shapes = [((rows // 2, 2 * DH), F32), ((rows // 2, DH), F32)]
        shapes += [((rows // 2, 2 * DH), BF16), ((rows // 2, DH), F32)]
        near = lambda i: (jnp.minimum(i, half - 1), 0)
        far = lambda i: (jnp.maximum(i - half, 0), 0)
        out_specs = [
            pl.BlockSpec((tile, s[1]), near if n < 2 else far) for n, (s, _) in enumerate(shapes)
        ]
    else:
        shapes = [((rows, 2 * DH), F32), ((rows, DH), F32)]
        out_specs = [row_block(2 * DH), row_block(DH)]
    return pl.pallas_call(
        functools.partial(attend_kernel, len(kvs), state is None, last, tiles),
        grid=(tiles,),
        in_specs=in_specs,
        out_specs=out_specs,
        out_shape=[jax.ShapeDtypeStruct(s, t) for s, t in shapes],
        scratch_shapes=[pltpu.VMEM((keys, 4 * DH), BF16)],
        compiler_params=params(48),
        cost_estimate=pl.CostEstimate(
            flops=2 * 8 * rows * keys * DH,
            bytes_accessed=keys * 4 * DH * 2 + rows * 4 * DH * 8,
            transcendentals=rows * keys,
        ),
        name="attend",
    )(*ins)


def join_kernel(mine, mine_stat, other, other_stat, primal, tangent, squares):
    top_a, top_b = mine_stat[:, 0:1], other_stat[:, 0:1]
    top = jnp.maximum(top_a, top_b)
    part_a, part_b = jnp.exp2(top_a - top), jnp.exp2(top_b - top)
    inverse = 1.0 / (part_a + part_b)
    part_a, part_b = part_a * inverse, part_b * inverse
    both = mine[...] * part_a + other[...].astype(F32) * part_b
    cross = mine_stat[:, 1:2] * part_a + other_stat[:, 1:2] * part_b
    out = both[:, :DH]
    moved = both[:, DH:] - cross * out
    primal[...] = out.astype(BF16)
    tangent[...] = moved
    squares[...] = lax.dot_general(
        jnp.ones((8, DH), F32),
        moved * moved,
        (((1,), (1,)), ((), ())),
        precision=lax.Precision.HIGHEST,
        preferred_element_type=F32,
    )


def join(mine, mine_stat, other, other_stat):
    rows = mine.shape[0]
    half = rows // 2
    row = lambda width: pl.BlockSpec((half, width), lambda i: (i, 0))
    return pl.pallas_call(
        join_kernel,
        grid=(2,),
        in_specs=[row(2 * DH), row(DH), row(2 * DH), row(DH)],
        out_specs=[row(DH), row(DH), pl.BlockSpec((8, half), lambda i: (0, i))],
        out_shape=[
            jax.ShapeDtypeStruct((rows, DH), BF16),
            jax.ShapeDtypeStruct((rows, DH), F32),
            jax.ShapeDtypeStruct((8, rows), F32),
        ],
        compiler_params=params(16),
        name="join",
    )(mine, mine_stat, other, other_stat)


def finish_kernel(primal, primal_in, tangent, tangent_in, square_a, square_b, square_c, square_d, attended, unit):
    flip = lax.axis_index("yh") == 1
    squares = square_a[...] + square_b[...] + square_c[...] + square_d[...]
    mean = lax.dot_general(
        squares,
        jnp.full((8, DH), 1.0 / (8 * HEADS * DH), F32),
        (((0,), (0,)), ((), ())),
        precision=lax.Precision.HIGHEST,
        preferred_element_type=F32,
    )
    inverse = 1.0 / jnp.sqrt(mean + 1e-06)
    mine, other = primal[...], primal_in[...]
    attended[:, :DH] = jnp.where(flip, other, mine)
    attended[:, DH:] = jnp.where(flip, mine, other)
    mine = (tangent[...] * inverse).astype(BF16)
    other = (tangent_in[...] * inverse).astype(BF16)
    unit[:, :DH] = jnp.where(flip, other, mine)
    unit[:, DH:] = jnp.where(flip, mine, other)


def finish(*arrays):
    rows = arrays[0].shape[0]
    out = jax.ShapeDtypeStruct((rows, 2 * DH), BF16)
    return pl.pallas_call(
        finish_kernel, out_shape=(out, out), compiler_params=params(16), name="finish"
    )(*arrays)


def shift(array, axis, count, by):
    return lax.ppermute(array, axis, [(i, (i + by) % count) for i in range(count)])


def on_device(ring, lanes, q, k, v, qt, kt, vt):
    tokens = q.shape[0]
    right = lambda a: shift(a, "z", ring, 1)
    left = lambda a: shift(a, "z", ring, -1)
    over_y = lambda a: lax.ppermute(a, "yh", SWAP)
    over_core = lambda a: lax.ppermute(a, "core", SWAP)

    kv_a, q_a, kv_other, q_other = pack(q, k, v, qt, kt, vt)
    q_b = over_y(q_other)
    kv_b = over_y(kv_other)
    query = jnp.concatenate([q_a, q_b, over_core(q_a), over_core(q_b)], axis=0)

    groups = [[kv_a, kv_b]]
    right_a, left_a, right_b, left_b = kv_a, kv_a, kv_b, kv_b
    for hop in range(1, ring // 2):
        right_a, left_a = right(right_a), left(left_a)
        right_b, left_b = right(right_b), left(left_b)
        groups.append([right_a, left_a, right_b, left_b])
    groups.append([right(right_a), left(left_b)])

    state = None
    for group in groups[:-1]:
        state = attend(query, group, state)
    near, near_stat, far, far_stat = attend(query, groups[-1], state, last=True)
    primal, tangent, squares = join(near, near_stat, over_core(far), over_core(far_stat))

    primal_in = over_y(primal[tokens:])
    tangent_in = over_y(tangent[tokens:])
    squares = squares + shift(squares, "x", lanes, 1) + shift(squares, "x", lanes, 2) + shift(squares, "x", lanes, 3)
    near_sq, far_sq = squares[:, :tokens], squares[:, tokens:]
    same = lax.ppermute(near_sq, "yl", SWAP)
    cross = over_y(far_sq)
    both = lax.ppermute(far_sq, ("yh", "yl"), ((0, 3), (3, 0), (1, 2), (2, 1)))
    return finish(primal[:tokens], primal_in, tangent[:tokens], tangent_in, near_sq, same, cross, both)


def solution(mesh):
    fine = Mesh(mesh.devices.reshape(2, -1, 2, 2, mesh.shape["head"] // 2), ("yh", "z", "core", "yl", "x"))
    spec = P(("yh", "z", "core"), ("yl", "x"))
    return jax.shard_map(
        functools.partial(on_device, fine.shape["z"], fine.shape["x"]),
        mesh=fine,
        in_specs=(spec,) * 6,
        out_specs=(spec, spec),
        check_vma=False,
    )
```

time: 557 us -> 117 us (0.21)
  waiting for transfers between devices: 352 us -> 21 us
  local copies, waits for them, and re-layouts: 89.7 us -> 9.18 us
  matrix products: 73.2 us -> 0 us
  starting transfers between devices: 0.15 us -> 43.3 us
  Pallas kernels: 0 us -> 41.3 us
  blocking collectives: 14.9 us -> 0 us
  between operations: 13.8 us -> 0.82 us
  other arithmetic: 8.63 us -> 0.01 us
    all_gather x4 -> x0, waiting for transfers between devices: 349 us -> none  [the longest x1 97 us: on_device(): lax.all_gather(key_proj, 'seq', axis=0, tiled=True)]
    dot_general x48 -> x0, matrix products: 73.2 us -> none  [the longest x24 30.6 us: apply_values(): jnp.einsum('htn,nhd->htd', weight_bf, value_block, preferred_element_type...]
    ppermute x0 -> x28, starting transfers between devices: none -> 43.3 us  [the longest x17 27.1 us: shift(): lax.ppermute(array, axis, [(i, (i + by) % count) for i in range(count)])]
    pallas_call x0 -> x8, Pallas kernels: none -> 41.3 us  [the longest x5 38.6 us: attend(): pl.pallas_call(functools.partial(attend_kernel, len(kvs), state is None,...]
    reshape x4 -> x0, local copies, waits for them, and re-layouts: 38.9 us -> none  [split_blocks(): return piece.reshape(length // block, block, head_count, DH)]
    dynamic_slice x16 -> x0, local copies, waits for them, and re-layouts: 35.9 us -> none  [on_device(): state, unused = lax.scan(inner, state, stacked)]
    ppermute x0 -> x28, waiting for transfers between devices: none -> 21 us  [the longest x17 10.1 us: shift(): lax.ppermute(array, axis, [(i, (i + by) % count) for i in range(count)])]
    psum x1 -> x0, blocking collectives: 14.9 us -> none  [on_device(): all_squares = lax.psum(local_squares, 'head')]
  transfers between devices with their start and end apart: 4 -> 28, of which waited for: 4 -> 9; matrix products, arithmetic and copies ran while one was open for 6% -> 0% of each run, Pallas kernels for 0% -> 28%
where the time goes in v1:
time: 117 us; the launch traced here: 116 us
  starting transfers between devices  43.3 us (37%)
  Pallas kernels  41.3 us (35%)
  waiting for transfers between devices  21 us (18%)
  local copies, waits for them, and re-layouts  9.18 us (8%)
    pallas_call x5, Pallas kernels, attend(): pl.pallas_call(functools.partial(attend_kernel, len(kvs), state is None,...  38.6 us
    ppermute x17, starting transfers between devices, shift(): lax.ppermute(array, axis, [(i, (i + by) % count) for i in range(count)])  27.1 us
    ppermute x17, waiting for transfers between devices, shift(): lax.ppermute(array, axis, [(i, (i + by) % count) for i in range(count)])  10.1 us
    ppermute x5, starting transfers between devices, on_device(): over_y = lambda a: lax.ppermute(a, 'yh', SWAP)  9.9 us
    unnamed x21, local copies, waits for them, and re-layouts  9.12 us
    ppermute x5, waiting for transfers between devices, on_device(): over_y = lambda a: lax.ppermute(a, 'yh', SWAP)  5.6 us
    ppermute x4, starting transfers between devices, on_device(): over_core = lambda a: lax.ppermute(a, 'core', SWAP)  4.97 us
  transfers between devices with their start and end apart: 28, of which 9 were waited for; matrix products, arithmetic and copies ran while one was open for 0% of the time, Pallas kernels for 28%

profile of v1, /device:TPU:1, one launch (start us, length us, event | category | flops | bytes accessed | tf_op | source)
XLA Modules:
  0.0 115.6 jit_solution(9468816083097168557)
XLA Ops:
  0.6 0.9 copy-done
  1.6 0.9 copy-done.1
  2.5 0.9 copy-done.2
  3.4 0.9 copy-done.3
  4.3 0.9 copy-done.4
  5.3 0.9 copy-done.5
  6.2 0.2 pack.1
  6.4 3.8 %collective-permute-start.7 = (bf16[384,512]{1,0:T(8,128)(2,1)S(1)}, bf16[384,512]{1,0:T(8,128)(2,1)S(1)}, u32[]{:S(2)}, u32[]{:S(2)}) collective-permute-start(bf16[384,512]{1,0:T(8,128)(2,1)S(1)} %get-tuple-element.24), channel_id=1, source_target_pairs={{0,128},{128,0},{1,129},{129,1},{2,130},{130,2},{3,131},{131,3},{4... | collective-permute-start | bytes 1179656 | tf_op jit(solution)/shard_map/ppermute | solution.py:237
  10.2 5.6 %collective-permute-start.12 = (bf16[384,512]{1,0:T(8,128)(2,1)S(1)}, bf16[384,512]{1,0:T(8,128)(2,1)S(1)}, u32[]{:S(2)}, u32[]{:S(2)}) collective-permute-start(bf16[384,512]{1,0:T(8,128)(2,1)S(1)} %get-tuple-element.23.refs_1_), channel_id=1, source_target_pairs={{0,112},{16,0},{32,16},{48,32},{64,48},{80,64},{96,80},{112,96},{1... | collective-permute-start | bytes 1179656 | tf_op jit(solution)/shard_map/ppermute | solution.py:230
  15.8 0.0 collective-permute-start.3
  15.8 0.1 collective-permute-start
  15.9 1.5 %collective-permute-start.1 = (bf16[384,256]{1,0:T(8,128)(2,1)S(1)}, bf16[384,256]{1,0:T(8,128)(2,1)S(1)}, u32[]{:S(2)}, u32[]{:S(2)}) collective-permute-start(bf16[384,256]{1,0:T(8,128)(2,1)S(1)} %get-tuple-element.21), channel_id=1, source_target_pairs={{0,8},{8,0},{1,9},{9,1},{2,10},{10,2},{3,11},{11,3},{4,12},{12,4},... | collective-permute-start | bytes 589832 | tf_op jit(solution)/shard_map/ppermute | solution.py:238
  17.4 5.1 %collective-permute-done = bf16[384,256]{1,0:T(8,128)(2,1)S(1)} collective-permute-done((bf16[384,256]{1,0:T(8,128)(2,1)S(1)}, bf16[384,256]{1,0:T(8,128)(2,1)S(1)}, u32[]{:S(2)}, u32[]{:S(2)}) %collective-permute-start) | collective-permute-done | bytes 196640 | tf_op jit(solution)/shard_map/ppermute | solution.py:237
  22.5 2.2 %collective-permute-start.2 = (bf16[384,256]{1,0:T(8,128)(2,1)S(1)}, bf16[384,256]{1,0:T(8,128)(2,1)S(1)}, u32[]{:S(2)}, u32[]{:S(2)}) collective-permute-start(bf16[384,256]{1,0:T(8,128)(2,1)S(1)} %collective-permute-done), channel_id=1, source_target_pairs={{0,8},{8,0},{1,9},{9,1},{2,10},{10,2},{3,11},{11,3},{4,12},{12,4},... | collective-permute-start | bytes 589832 | tf_op jit(solution)/shard_map/ppermute | solution.py:238
  24.7 0.0 collective-permute-done.7.refs_2_
  24.7 1.6 %collective-permute-start.15 = (bf16[384,512]{1,0:T(8,128)(2,1)S(1)}, bf16[384,512]{1,0:T(8,128)(2,1)S(1)}, u32[]{:S(2)}, u32[]{:S(2)}) collective-permute-start(bf16[384,512]{1,0:T(8,128)(2,1)S(1)} %collective-permute-done.7.refs_2_), channel_id=1, source_target_pairs={{0,16},{16,32},{32,48},{48,64},{64,80},{80,96},{96,112},{112,0},{1... | collective-permute-start | bytes 1179656 | tf_op jit(solution)/shard_map/ppermute | solution.py:230
  26.3 0.0 collective-permute-done.1
  26.3 4.0 %collective-permute-start.8 = (bf16[384,512]{1,0:T(8,128)(2,1)S(1)}, bf16[384,512]{1,0:T(8,128)(2,1)S(1)}, u32[]{:S(2)}, u32[]{:S(2)}) collective-permute-start(bf16[384,512]{1,0:T(8,128)(2,1)S(1)} %collective-permute-done.7.refs_2_), channel_id=1, source_target_pairs={{0,112},{16,0},{32,16},{48,32},{64,48},{80,64},{96,80},{112,96},{1... | collective-permute-start | bytes 1179656 | tf_op jit(solution)/shard_map/ppermute | solution.py:230
  30.4 0.0 collective-permute-done.12.refs_2_
  30.4 1.4 %collective-permute-start.13 = (bf16[384,512]{1,0:T(8,128)(2,1)S(1)}, bf16[384,512]{1,0:T(8,128)(2,1)S(1)}, u32[]{:S(2)}, u32[]{:S(2)}) collective-permute-start(bf16[384,512]{1,0:T(8,128)(2,1)S(1)} %collective-permute-done.12.refs_2_), channel_id=1, source_target_pairs={{0,112},{16,0},{32,16},{48,32},{64,48},{80,64},{96,80},{112,96},{1... | collective-permute-start | bytes 1179656 | tf_op jit(solution)/shard_map/ppermute | solution.py:230
  31.7 0.0 collective-permute-done.3.refs_1_
  31.7 0.1 collective-permute-start.4
  31.9 0.0 collective-permute-done.2
  31.9 4.6 %attend.5 = (f32[1536,256]{1,0:T(8,128)S(1)}, f32[1536,128]{1,0:T(8,128)S(1)}) custom-call(bf16[1536,256]{1,0:T(8,128)(2,1)S(1)} %constant_dynamic-update-slice_fusion.refs_0_, bf16[384,512]{1,0:T(8,128)(2,1)S(1)} %get-tuple-element.23.refs_1_, bf16[384,512]{1,0:T(8,128)(2,1)S(1)} %collective-permute-done.7.refs_2_), custom_call_target="tpu_custom_call" | custom-call | flops 2415919104 | bytes 7077888 | tf_op jit(solution)/shard_map/attend/pallas_call | solution.py:144
  36.5 1.2 %copy-done.6 = f32[1536,256]{1,0:T(8,128)} copy-done((f32[1536,256]{1,0:T(8,128)}, f32[1536,256]{1,0:T(8,128)S(1)}, u32[]{:S(2)}) %copy-start.6) | copy-done | bytes 1572888
  37.7 2.1 %collective-permute-done.15.refs_3_ = bf16[384,512]{1,0:T(8,128)(2,1)S(1)} collective-permute-done((bf16[384,512]{1,0:T(8,128)(2,1)S(1)}, bf16[384,512]{1,0:T(8,128)(2,1)S(1)}, u32[]{:S(2)}, u32[]{:S(2)}) %collective-permute-start.15) | collective-permute-done | bytes 393248 | tf_op jit(solution)/shard_map/ppermute | solution.py:230
  39.8 0.0 collective-permute-start.16
  39.8 0.0 collective-permute-done.8.refs_4_
  39.8 2.7 %collective-permute-start.9 = (bf16[384,512]{1,0:T(8,128)(2,1)S(1)}, bf16[384,512]{1,0:T(8,128)(2,1)S(1)}, u32[]{:S(2)}, u32[]{:S(2)}) collective-permute-start(bf16[384,512]{1,0:T(8,128)(2,1)S(1)} %collective-permute-done.8.refs_4_), channel_id=1, source_target_pairs={{0,112},{16,0},{32,16},{48,32},{64,48},{80,64},{96,80},{112,96},{1... | collective-permute-start | bytes 1179656 | tf_op jit(solution)/shard_map/ppermute | solution.py:230
  42.4 5.7 %collective-permute-done.4.refs_1_ = bf16[384,512]{1,0:T(8,128)(2,1)S(1)} collective-permute-done((bf16[384,512]{1,0:T(8,128)(2,1)S(1)}, bf16[384,512]{1,0:T(8,128)(2,1)S(1)}, u32[]{:S(2)}, u32[]{:S(2)}) %collective-permute-start.4) | collective-permute-done | bytes 393248 | tf_op jit(solution)/shard_map/ppermute | solution.py:230
  48.2 2.7 %collective-permute-start.14 = (bf16[384,512]{1,0:T(8,128)(2,1)S(1)}, bf16[384,512]{1,0:T(8,128)(2,1)S(1)}, u32[]{:S(2)}, u32[]{:S(2)}) collective-permute-start(bf16[384,512]{1,0:T(8,128)(2,1)S(1)} %collective-permute-done.13.refs_2_), channel_id=1, source_target_pairs={{0,112},{16,0},{32,16},{48,32},{64,48},{80,64},{96,80},{112,96},{1... | collective-permute-start | bytes 1179656 | tf_op jit(solution)/shard_map/ppermute | solution.py:230
  50.9 9.3 %attend.6 = (f32[1536,256]{1,0:T(8,128)S(1)}, f32[1536,128]{1,0:T(8,128)S(1)}) custom-call(bf16[1536,256]{1,0:T(8,128)(2,1)S(1)} %constant_dynamic-update-slice_fusion.refs_0_, bf16[384,512]{1,0:T(8,128)(2,1)S(1)} %collective-permute-done.3.refs_1_, bf16[384,512]{1,0:T(8,128)(2,1)S(1)} %collective-permute-done.12.refs_2_, ...), custom_call_target="tpu_custom_call" | custom-call | flops 4831838208 | bytes 7864320 | tf_op jit(solution)/shard_map/attend/pallas_call | solution.py:144
  60.2 1.2 %copy-done.7 = f32[1536,256]{1,0:T(8,128)} copy-done((f32[1536,256]{1,0:T(8,128)}, f32[1536,256]{1,0:T(8,128)S(1)}, u32[]{:S(2)}) %copy-start.7) | copy-done | bytes 1572888
  61.3 0.0 collective-permute-done.9.refs_4_
  61.3 0.1 collective-permute-start.10
  61.4 1.4 %collective-permute-start.17 = (bf16[384,512]{1,0:T(8,128)(2,1)S(1)}, bf16[384,512]{1,0:T(8,128)(2,1)S(1)}, u32[]{:S(2)}, u32[]{:S(2)}) collective-permute-start(bf16[384,512]{1,0:T(8,128)(2,1)S(1)} %collective-permute-done.16.refs_3_), channel_id=1, source_target_pairs={{0,16},{16,32},{32,48},{48,64},{64,80},{80,96},{96,112},{112,0},{1... | collective-permute-start | bytes 1179656 | tf_op jit(solution)/shard_map/ppermute | solution.py:230
  62.8 2.2 %collective-permute-done.5.refs_1_ = bf16[384,512]{1,0:T(8,128)(2,1)S(1)} collective-permute-done((bf16[384,512]{1,0:T(8,128)(2,1)S(1)}, bf16[384,512]{1,0:T(8,128)(2,1)S(1)}, u32[]{:S(2)}, u32[]{:S(2)}) %collective-permute-start.5) | collective-permute-done | bytes 393248 | tf_op jit(solution)/shard_map/ppermute | solution.py:230
  65.0 9.3 %attend.7 = (f32[1536,256]{1,0:T(8,128)S(1)}, f32[1536,128]{1,0:T(8,128)S(1)}) custom-call(bf16[1536,256]{1,0:T(8,128)(2,1)S(1)} %constant_dynamic-update-slice_fusion.refs_0_, bf16[384,512]{1,0:T(8,128)(2,1)S(1)} %collective-permute-done.4.refs_1_, bf16[384,512]{1,0:T(8,128)(2,1)S(1)} %collective-permute-done.13.refs_2_, ...), custom_call_target="tpu_custom_call" | custom-call | flops 4831838208 | bytes 7864320 | tf_op jit(solution)/shard_map/attend/pallas_call | solution.py:144
  74.3 1.2 %copy-done.8 = f32[1536,256]{1,0:T(8,128)} copy-done((f32[1536,256]{1,0:T(8,128)}, f32[1536,256]{1,0:T(8,128)S(1)}, u32[]{:S(2)}) %copy-start.8) | copy-done | bytes 1572888
  75.5 0.0 collective-permute-done.10.refs_4_
  75.5 2.7 %collective-permute-start.11 = (bf16[384,512]{1,0:T(8,128)(2,1)S(1)}, bf16[384,512]{1,0:T(8,128)(2,1)S(1)}, u32[]{:S(2)}, u32[]{:S(2)}) collective-permute-start(bf16[384,512]{1,0:T(8,128)(2,1)S(1)} %collective-permute-done.10.refs_4_), channel_id=1, source_target_pairs={{0,112},{16,0},{32,16},{48,32},{64,48},{80,64},{96,80},{112,96},{1... | collective-permute-start | bytes 1179656 | tf_op jit(solution)/shard_map/ppermute | solution.py:230
  78.2 9.3 %attend.8 = (f32[1536,256]{1,0:T(8,128)S(1)}, f32[1536,128]{1,0:T(8,128)S(1)}) custom-call(bf16[1536,256]{1,0:T(8,128)(2,1)S(1)} %constant_dynamic-update-slice_fusion.refs_0_, bf16[384,512]{1,0:T(8,128)(2,1)S(1)} %collective-permute-done.5.refs_1_, bf16[384,512]{1,0:T(8,128)(2,1)S(1)} %collective-permute-done.14.refs_2_, ...), custom_call_target="tpu_custom_call" | custom-call | flops 4831838208 | bytes 7864320 | tf_op jit(solution)/shard_map/attend/pallas_call | solution.py:144
  87.5 0.0 collective-permute-done.11.refs_2_
  87.5 6.1 %attend.9 = (f32[768,256]{1,0:T(8,128)S(1)}, f32[768,128]{1,0:T(8,128)S(1)}, bf16[768,256]{1,0:T(8,128)(2,1)S(1)}, f32[768,128]{1,0:T(8,128)S(1)}) custom-call(bf16[1536,256]{1,0:T(8,128)(2,1)S(1)} %constant_dynamic-update-slice_fusion.refs_0_, bf16[384,512]{1,0:T(8,128)(2,1)S(1)} %collective-permute-done.6.refs_1_, ...), custom_call_target="tpu_custom_call" | custom-call | flops 2415919104 | bytes 7077888 | tf_op jit(solution)/shard_map/attend/pallas_call | solution.py:144
  93.7 1.2 %collective-permute-start.18 = (bf16[768,256]{1,0:T(8,128)(2,1)S(1)}, bf16[768,256]{1,0:T(8,128)(2,1)S(1)}, u32[]{:S(2)}, u32[]{:S(2)}) collective-permute-start(bf16[768,256]{1,0:T(8,128)(2,1)S(1)} %get-tuple-element.35), channel_id=1, source_target_pairs={{0,8},{8,0},{1,9},{9,1},{2,10},{10,2},{3,11},{11,3},{4,12},{12,4},... | collective-permute-start | bytes 1179656 | tf_op jit(solution)/shard_map/ppermute | solution.py:238
  94.9 0.1 collective-permute-start.19
  95.0 1.2 %collective-permute-done.18.other = bf16[768,256]{1,0:T(8,128)(2,1)S(1)} collective-permute-done((bf16[768,256]{1,0:T(8,128)(2,1)S(1)}, bf16[768,256]{1,0:T(8,128)(2,1)S(1)}, u32[]{:S(2)}, u32[]{:S(2)}) %collective-permute-start.18) | collective-permute-done | bytes 393248 | tf_op jit(solution)/shard_map/ppermute | solution.py:238
  96.2 0.6 collective-permute-done.19.other_stat
  96.8 1.3 %join.1 = (bf16[768,128]{1,0:T(8,128)(2,1)S(1)}, f32[768,128]{1,0:T(8,128)S(1)}, f32[8,768]{1,0:T(8,128)S(1)}) custom-call(f32[768,256]{1,0:T(8,128)S(1)} %get-tuple-element.33.mine, f32[768,128]{1,0:T(8,128)S(1)} %get-tuple-element.34.mine_stat, bf16[768,256]{1,0:T(8,128)(2,1)S(1)} %collective-permute-done.18.other, ...), custom_call_target="tpu_custom_call" | custom-call | tf_op jit(solution)/shard_map/join/pallas_call | solution.py:186
  98.1 1.2 %collective-permute-start.22 = (f32[8,768]{1,0:T(8,128)S(1)}, f32[8,768]{1,0:T(8,128)S(1)}, u32[]{:S(2)}, u32[]{:S(2)}) collective-permute-start(f32[8,768]{1,0:T(8,128)S(1)} %get-tuple-element.39), channel_id=1, source_target_pairs={{0,1},{1,2},{2,3},{3,0},{4,5},{5,6},{6,7},{7,4},{8,9},{9,10},{10,1... | collective-permute-start | bytes 73736 | tf_op jit(solution)/shard_map/ppermute | solution.py:230
  99.3 2.5 %collective-permute-start.23 = (f32[8,768]{1,0:T(8,128)S(1)}, f32[8,768]{1,0:T(8,128)S(1)}, u32[]{:S(2)}, u32[]{:S(2)}) collective-permute-start(f32[8,768]{1,0:T(8,128)S(1)} %get-tuple-element.39), channel_id=1, source_target_pairs={{0,2},{1,3},{2,0},{3,1},{4,6},{5,7},{6,4},{7,5},{8,10},{9,11},{10,... | collective-permute-start | bytes 73736 | tf_op jit(solution)/shard_map/ppermute | solution.py:230
  101.8 1.2 %collective-permute-start.24 = (f32[8,768]{1,0:T(8,128)S(1)}, f32[8,768]{1,0:T(8,128)S(1)}, u32[]{:S(2)}, u32[]{:S(2)}) collective-permute-start(f32[8,768]{1,0:T(8,128)S(1)} %get-tuple-element.39), channel_id=1, source_target_pairs={{0,3},{1,0},{2,1},{3,2},{4,7},{5,4},{6,5},{7,6},{8,11},{9,8},{10,9... | collective-permute-start | bytes 73736 | tf_op jit(solution)/shard_map/ppermute | solution.py:230
  102.9 3.2 %collective-permute-start.21 = (f32[384,128]{1,0:T(8,128)S(1)}, f32[384,128]{1,0:T(8,128)S(1)}, u32[]{:S(2)}, u32[]{:S(2)}) collective-permute-start(f32[384,128]{1,0:T(8,128)S(1)} %get-tuple-element.40), channel_id=1, source_target_pairs={{0,128},{128,0},{1,129},{129,1},{2,130},{130,2},{3,131},{131,3},{4... | collective-permute-start | bytes 589832 | tf_op jit(solution)/shard_map/ppermute | solution.py:237
  106.2 0.1 collective-permute-start.20
  106.3 0.0 collective-permute-done.22
  106.4 1.4 %collective-permute-start.25 = (f32[8,384]{1,0:T(8,128)S(1)}, f32[8,384]{1,0:T(8,128)S(1)}, u32[]{:S(2)}, u32[]{:S(2)}) collective-permute-start(f32[8,384]{1,0:T(8,128)S(1)} %get-tuple-element.45.square_a), channel_id=1, source_target_pairs={{0,4},{4,0},{1,5},{5,1},{2,6},{6,2},{3,7},{7,3},{8,12},{12,8},{9,1... | collective-permute-start | bytes 36872 | tf_op jit(solution)/shard_map/ppermute | solution.py:263
  107.8 2.6 %collective-permute-start.26 = (f32[8,384]{1,0:T(8,128)S(1)}, f32[8,384]{1,0:T(8,128)S(1)}, u32[]{:S(2)}, u32[]{:S(2)}) collective-permute-start(f32[8,384]{1,0:T(8,128)S(1)} %get-tuple-element.44), channel_id=1, source_target_pairs={{0,128},{128,0},{1,129},{129,1},{2,130},{130,2},{3,131},{131,3},{4... | collective-permute-start | bytes 36872 | tf_op jit(solution)/shard_map/ppermute | solution.py:237
  110.4 0.0 collective-permute-start.27
  110.4 2.3 %collective-permute-done.25.square_b = f32[8,384]{1,0:T(8,128)S(1)} collective-permute-done((f32[8,384]{1,0:T(8,128)S(1)}, f32[8,384]{1,0:T(8,128)S(1)}, u32[]{:S(2)}, u32[]{:S(2)}) %collective-permute-start.25) | collective-permute-done | bytes 12320 | tf_op jit(solution)/shard_map/ppermute | solution.py:263
  112.6 0.5 collective-permute-done.26.square_c
  113.2 1.3 %collective-permute-done.27.square_d = f32[8,384]{1,0:T(8,128)S(1)} collective-permute-done((f32[8,384]{1,0:T(8,128)S(1)}, f32[8,384]{1,0:T(8,128)S(1)}, u32[]{:S(2)}, u32[]{:S(2)}) %collective-permute-start.27) | collective-permute-done | bytes 12320 | tf_op jit(solution)/shard_map/ppermute | solution.py:265
  114.4 0.0 collective-permute-done.20.primal_in
  114.4 0.0 collective-permute-done.21.tangent_in
  114.4 1.2 %finish.1 = (bf16[384,256]{1,0:T(8,128)(2,1)}, bf16[384,256]{1,0:T(8,128)(2,1)}) custom-call(bf16[384,128]{1,0:T(8,128)(2,1)S(1)} %get-tuple-element.43.primal, bf16[384,128]{1,0:T(8,128)(2,1)S(1)} %collective-permute-done.20.primal_in, f32[384,128]{1,0:T(8,128)S(1)} %get-tuple-element.41.tangent, f32[384,128]{1,0:T(8,128)S(1)} %collective-permute-done.21.tangent_in, ...), custom_call_target="tpu_custom_call" | custom-call | tf_op jit(solution)/shard_map/finish/pallas_call | solution.py:224
  (26 shorter events, 0.2 us)
Async XLA Ops:
  0.6 0.9 copy-start
  1.6 0.9 copy-start.1
  2.5 0.9 copy-start.2
  3.4 0.9 copy-start.3
  4.3 0.9 copy-start.4
  5.3 0.9 copy-start.5
  6.4 18.3 %collective-permute-start.7 = (bf16[384,512]{1,0:T(8,128)(2,1)S(1)}, bf16[384,512]{1,0:T(8,128)(2,1)S(1)}, u32[]{:S(2)}, u32[]{:S(2)}) collective-permute-start(bf16[384,512]{1,0:T(8,128)(2,1)S(1)} %get-tuple-element.24), channel_id=1, source_target_pairs={{0,128},{128,0},{1,129},{129,1},{2,130},{130,2},{3,131},{131,3},{4... | collective-permute-start | bytes 1179656 | tf_op jit(solution)/shard_map/ppermute | solution.py:237
  10.2 20.1 %collective-permute-start.12 = (bf16[384,512]{1,0:T(8,128)(2,1)S(1)}, bf16[384,512]{1,0:T(8,128)(2,1)S(1)}, u32[]{:S(2)}, u32[]{:S(2)}) collective-permute-start(bf16[384,512]{1,0:T(8,128)(2,1)S(1)} %get-tuple-element.23.refs_1_), channel_id=1, source_target_pairs={{0,112},{16,0},{32,16},{48,32},{64,48},{80,64},{96,80},{112,96},{1... | collective-permute-start | bytes 1179656 | tf_op jit(solution)/shard_map/ppermute | solution.py:230
  15.8 15.9 %collective-permute-start.3 = (bf16[384,512]{1,0:T(8,128)(2,1)S(1)}, bf16[384,512]{1,0:T(8,128)(2,1)S(1)}, u32[]{:S(2)}, u32[]{:S(2)}) collective-permute-start(bf16[384,512]{1,0:T(8,128)(2,1)S(1)} %get-tuple-element.23.refs_1_), channel_id=1, source_target_pairs={{0,16},{16,32},{32,48},{48,64},{64,80},{80,96},{96,112},{112,0},{1... | collective-permute-start | bytes 1179656 | tf_op jit(solution)/shard_map/ppermute | solution.py:230
  15.8 6.7 %collective-permute-start = (bf16[384,256]{1,0:T(8,128)(2,1)S(1)}, bf16[384,256]{1,0:T(8,128)(2,1)S(1)}, u32[]{:S(2)}, u32[]{:S(2)}) collective-permute-start(bf16[384,256]{1,0:T(8,128)(2,1)S(1)} %get-tuple-element.22), channel_id=1, source_target_pairs={{0,128},{128,0},{1,129},{129,1},{2,130},{130,2},{3,131},{131,3},{4... | collective-permute-start | bytes 589832 | tf_op jit(solution)/shard_map/ppermute | solution.py:237
  15.9 10.4 %collective-permute-start.1 = (bf16[384,256]{1,0:T(8,128)(2,1)S(1)}, bf16[384,256]{1,0:T(8,128)(2,1)S(1)}, u32[]{:S(2)}, u32[]{:S(2)}) collective-permute-start(bf16[384,256]{1,0:T(8,128)(2,1)S(1)} %get-tuple-element.21), channel_id=1, source_target_pairs={{0,8},{8,0},{1,9},{9,1},{2,10},{10,2},{3,11},{11,3},{4,12},{12,4},... | collective-permute-start | bytes 589832 | tf_op jit(solution)/shard_map/ppermute | solution.py:238
  22.5 9.4 %collective-permute-start.2 = (bf16[384,256]{1,0:T(8,128)(2,1)S(1)}, bf16[384,256]{1,0:T(8,128)(2,1)S(1)}, u32[]{:S(2)}, u32[]{:S(2)}) collective-permute-start(bf16[384,256]{1,0:T(8,128)(2,1)S(1)} %collective-permute-done), channel_id=1, source_target_pairs={{0,8},{8,0},{1,9},{9,1},{2,10},{10,2},{3,11},{11,3},{4,12},{12,4},... | collective-permute-start | bytes 589832 | tf_op jit(solution)/shard_map/ppermute | solution.py:238
  24.7 15.1 %collective-permute-start.15 = (bf16[384,512]{1,0:T(8,128)(2,1)S(1)}, bf16[384,512]{1,0:T(8,128)(2,1)S(1)}, u32[]{:S(2)}, u32[]{:S(2)}) collective-permute-start(bf16[384,512]{1,0:T(8,128)(2,1)S(1)} %collective-permute-done.7.refs_2_), channel_id=1, source_target_pairs={{0,16},{16,32},{32,48},{48,64},{64,80},{80,96},{96,112},{112,0},{1... | collective-permute-start | bytes 1179656 | tf_op jit(solution)/shard_map/ppermute | solution.py:230
  26.3 13.4 %collective-permute-start.8 = (bf16[384,512]{1,0:T(8,128)(2,1)S(1)}, bf16[384,512]{1,0:T(8,128)(2,1)S(1)}, u32[]{:S(2)}, u32[]{:S(2)}) collective-permute-start(bf16[384,512]{1,0:T(8,128)(2,1)S(1)} %collective-permute-done.7.refs_2_), channel_id=1, source_target_pairs={{0,112},{16,0},{32,16},{48,32},{64,48},{80,64},{96,80},{112,96},{1... | collective-permute-start | bytes 1179656 | tf_op jit(solution)/shard_map/ppermute | solution.py:230
  30.4 17.8 %collective-permute-start.13 = (bf16[384,512]{1,0:T(8,128)(2,1)S(1)}, bf16[384,512]{1,0:T(8,128)(2,1)S(1)}, u32[]{:S(2)}, u32[]{:S(2)}) collective-permute-start(bf16[384,512]{1,0:T(8,128)(2,1)S(1)} %collective-permute-done.12.refs_2_), channel_id=1, source_target_pairs={{0,112},{16,0},{32,16},{48,32},{64,48},{80,64},{96,80},{112,96},{1... | collective-permute-start | bytes 1179656 | tf_op jit(solution)/shard_map/ppermute | solution.py:230
  31.7 16.4 %collective-permute-start.4 = (bf16[384,512]{1,0:T(8,128)(2,1)S(1)}, bf16[384,512]{1,0:T(8,128)(2,1)S(1)}, u32[]{:S(2)}, u32[]{:S(2)}) collective-permute-start(bf16[384,512]{1,0:T(8,128)(2,1)S(1)} %collective-permute-done.3.refs_1_), channel_id=1, source_target_pairs={{0,16},{16,32},{32,48},{48,64},{64,80},{80,96},{96,112},{112,0},{1... | collective-permute-start | bytes 1179656 | tf_op jit(solution)/shard_map/ppermute | solution.py:230
  36.5 1.2 %copy-start.6 = (f32[1536,256]{1,0:T(8,128)}, f32[1536,256]{1,0:T(8,128)S(1)}, u32[]{:S(2)}) copy-start(f32[1536,256]{1,0:T(8,128)S(1)} %get-tuple-element.25.refs_5_) | copy-start | bytes 4718596
  39.8 21.6 %collective-permute-start.16 = (bf16[384,512]{1,0:T(8,128)(2,1)S(1)}, bf16[384,512]{1,0:T(8,128)(2,1)S(1)}, u32[]{:S(2)}, u32[]{:S(2)}) collective-permute-start(bf16[384,512]{1,0:T(8,128)(2,1)S(1)} %collective-permute-done.15.refs_3_), channel_id=1, source_target_pairs={{0,16},{16,32},{32,48},{48,64},{64,80},{80,96},{96,112},{112,0},{1... | collective-permute-start | bytes 1179656 | tf_op jit(solution)/shard_map/ppermute | solution.py:230
  39.8 21.6 %collective-permute-start.9 = (bf16[384,512]{1,0:T(8,128)(2,1)S(1)}, bf16[384,512]{1,0:T(8,128)(2,1)S(1)}, u32[]{:S(2)}, u32[]{:S(2)}) collective-permute-start(bf16[384,512]{1,0:T(8,128)(2,1)S(1)} %collective-permute-done.8.refs_4_), channel_id=1, source_target_pairs={{0,112},{16,0},{32,16},{48,32},{64,48},{80,64},{96,80},{112,96},{1... | collective-permute-start | bytes 1179656 | tf_op jit(solution)/shard_map/ppermute | solution.py:230
  48.2 16.9 %collective-permute-start.5 = (bf16[384,512]{1,0:T(8,128)(2,1)S(1)}, bf16[384,512]{1,0:T(8,128)(2,1)S(1)}, u32[]{:S(2)}, u32[]{:S(2)}) collective-permute-start(bf16[384,512]{1,0:T(8,128)(2,1)S(1)} %collective-permute-done.4.refs_1_), channel_id=1, source_target_pairs={{0,16},{16,32},{32,48},{48,64},{64,80},{80,96},{96,112},{112,0},{1... | collective-permute-start | bytes 1179656 | tf_op jit(solution)/shard_map/ppermute | solution.py:230
  48.2 30.0 %collective-permute-start.14 = (bf16[384,512]{1,0:T(8,128)(2,1)S(1)}, bf16[384,512]{1,0:T(8,128)(2,1)S(1)}, u32[]{:S(2)}, u32[]{:S(2)}) collective-permute-start(bf16[384,512]{1,0:T(8,128)(2,1)S(1)} %collective-permute-done.13.refs_2_), channel_id=1, source_target_pairs={{0,112},{16,0},{32,16},{48,32},{64,48},{80,64},{96,80},{112,96},{1... | collective-permute-start | bytes 1179656 | tf_op jit(solution)/shard_map/ppermute | solution.py:230
  60.2 1.2 %copy-start.7 = (f32[1536,256]{1,0:T(8,128)}, f32[1536,256]{1,0:T(8,128)S(1)}, u32[]{:S(2)}) copy-start(f32[1536,256]{1,0:T(8,128)S(1)} %get-tuple-element.27.refs_5_) | copy-start | bytes 4718596
  61.3 14.2 %collective-permute-start.10 = (bf16[384,512]{1,0:T(8,128)(2,1)S(1)}, bf16[384,512]{1,0:T(8,128)(2,1)S(1)}, u32[]{:S(2)}, u32[]{:S(2)}) collective-permute-start(bf16[384,512]{1,0:T(8,128)(2,1)S(1)} %collective-permute-done.9.refs_4_), channel_id=1, source_target_pairs={{0,112},{16,0},{32,16},{48,32},{64,48},{80,64},{96,80},{112,96},{1... | collective-permute-start | bytes 1179656 | tf_op jit(solution)/shard_map/ppermute | solution.py:230
  61.4 16.8 %collective-permute-start.17 = (bf16[384,512]{1,0:T(8,128)(2,1)S(1)}, bf16[384,512]{1,0:T(8,128)(2,1)S(1)}, u32[]{:S(2)}, u32[]{:S(2)}) collective-permute-start(bf16[384,512]{1,0:T(8,128)(2,1)S(1)} %collective-permute-done.16.refs_3_), channel_id=1, source_target_pairs={{0,16},{16,32},{32,48},{48,64},{64,80},{80,96},{96,112},{112,0},{1... | collective-permute-start | bytes 1179656 | tf_op jit(solution)/shard_map/ppermute | solution.py:230
  65.0 22.5 %collective-permute-start.6 = (bf16[384,512]{1,0:T(8,128)(2,1)S(1)}, bf16[384,512]{1,0:T(8,128)(2,1)S(1)}, u32[]{:S(2)}, u32[]{:S(2)}) collective-permute-start(bf16[384,512]{1,0:T(8,128)(2,1)S(1)} %collective-permute-done.5.refs_1_), channel_id=1, source_target_pairs={{0,16},{16,32},{32,48},{48,64},{64,80},{80,96},{96,112},{112,0},{1... | collective-permute-start | bytes 1179656 | tf_op jit(solution)/shard_map/ppermute | solution.py:230
  74.3 1.2 %copy-start.8 = (f32[1536,256]{1,0:T(8,128)}, f32[1536,256]{1,0:T(8,128)S(1)}, u32[]{:S(2)}) copy-start(f32[1536,256]{1,0:T(8,128)S(1)} %get-tuple-element.29.refs_5_) | copy-start | bytes 4718596
  75.5 12.0 %collective-permute-start.11 = (bf16[384,512]{1,0:T(8,128)(2,1)S(1)}, bf16[384,512]{1,0:T(8,128)(2,1)S(1)}, u32[]{:S(2)}, u32[]{:S(2)}) collective-permute-start(bf16[384,512]{1,0:T(8,128)(2,1)S(1)} %collective-permute-done.10.refs_4_), channel_id=1, source_target_pairs={{0,112},{16,0},{32,16},{48,32},{64,48},{80,64},{96,80},{112,96},{1... | collective-permute-start | bytes 1179656 | tf_op jit(solution)/shard_map/ppermute | solution.py:230
  93.7 2.6 %collective-permute-start.18 = (bf16[768,256]{1,0:T(8,128)(2,1)S(1)}, bf16[768,256]{1,0:T(8,128)(2,1)S(1)}, u32[]{:S(2)}, u32[]{:S(2)}) collective-permute-start(bf16[768,256]{1,0:T(8,128)(2,1)S(1)} %get-tuple-element.35), channel_id=1, source_target_pairs={{0,8},{8,0},{1,9},{9,1},{2,10},{10,2},{3,11},{11,3},{4,12},{12,4},... | collective-permute-start | bytes 1179656 | tf_op jit(solution)/shard_map/ppermute | solution.py:238
  94.9 1.9 %collective-permute-start.19 = (f32[768,128]{1,0:T(8,128)S(1)}, f32[768,128]{1,0:T(8,128)S(1)}, u32[]{:S(2)}, u32[]{:S(2)}) collective-permute-start(f32[768,128]{1,0:T(8,128)S(1)} %get-tuple-element.36), channel_id=1, source_target_pairs={{0,8},{8,0},{1,9},{9,1},{2,10},{10,2},{3,11},{11,3},{4,12},{12,4},... | collective-permute-start | bytes 1179656 | tf_op jit(solution)/shard_map/ppermute | solution.py:238
  98.1 8.3 %collective-permute-start.22 = (f32[8,768]{1,0:T(8,128)S(1)}, f32[8,768]{1,0:T(8,128)S(1)}, u32[]{:S(2)}, u32[]{:S(2)}) collective-permute-start(f32[8,768]{1,0:T(8,128)S(1)} %get-tuple-element.39), channel_id=1, source_target_pairs={{0,1},{1,2},{2,3},{3,0},{4,5},{5,6},{6,7},{7,4},{8,9},{9,10},{10,1... | collective-permute-start | bytes 73736 | tf_op jit(solution)/shard_map/ppermute | solution.py:230
  99.3 7.0 %collective-permute-start.23 = (f32[8,768]{1,0:T(8,128)S(1)}, f32[8,768]{1,0:T(8,128)S(1)}, u32[]{:S(2)}, u32[]{:S(2)}) collective-permute-start(f32[8,768]{1,0:T(8,128)S(1)} %get-tuple-element.39), channel_id=1, source_target_pairs={{0,2},{1,3},{2,0},{3,1},{4,6},{5,7},{6,4},{7,5},{8,10},{9,11},{10,... | collective-permute-start | bytes 73736 | tf_op jit(solution)/shard_map/ppermute | solution.py:230
  101.8 4.6 %collective-permute-start.24 = (f32[8,768]{1,0:T(8,128)S(1)}, f32[8,768]{1,0:T(8,128)S(1)}, u32[]{:S(2)}, u32[]{:S(2)}) collective-permute-start(f32[8,768]{1,0:T(8,128)S(1)} %get-tuple-element.39), channel_id=1, source_target_pairs={{0,3},{1,0},{2,1},{3,2},{4,7},{5,4},{6,5},{7,6},{8,11},{9,8},{10,9... | collective-permute-start | bytes 73736 | tf_op jit(solution)/shard_map/ppermute | solution.py:230
  102.9 11.5 %collective-permute-start.21 = (f32[384,128]{1,0:T(8,128)S(1)}, f32[384,128]{1,0:T(8,128)S(1)}, u32[]{:S(2)}, u32[]{:S(2)}) collective-permute-start(f32[384,128]{1,0:T(8,128)S(1)} %get-tuple-element.40), channel_id=1, source_target_pairs={{0,128},{128,0},{1,129},{129,1},{2,130},{130,2},{3,131},{131,3},{4... | collective-permute-start | bytes 589832 | tf_op jit(solution)/shard_map/ppermute | solution.py:237
  106.2 8.2 %collective-permute-start.20 = (bf16[384,128]{1,0:T(8,128)(2,1)S(1)}, bf16[384,128]{1,0:T(8,128)(2,1)S(1)}, u32[]{:S(2)}, u32[]{:S(2)}) collective-permute-start(bf16[384,128]{1,0:T(8,128)(2,1)S(1)} %get-tuple-element.42), channel_id=1, source_target_pairs={{0,128},{128,0},{1,129},{129,1},{2,130},{130,2},{3,131},{131,3},{4... | collective-permute-start | bytes 294920 | tf_op jit(solution)/shard_map/ppermute | solution.py:237
  106.4 6.3 %collective-permute-start.25 = (f32[8,384]{1,0:T(8,128)S(1)}, f32[8,384]{1,0:T(8,128)S(1)}, u32[]{:S(2)}, u32[]{:S(2)}) collective-permute-start(f32[8,384]{1,0:T(8,128)S(1)} %get-tuple-element.45.square_a), channel_id=1, source_target_pairs={{0,4},{4,0},{1,5},{5,1},{2,6},{6,2},{3,7},{7,3},{8,12},{12,8},{9,1... | collective-permute-start | bytes 36872 | tf_op jit(solution)/shard_map/ppermute | solution.py:263
  107.8 5.4 %collective-permute-start.26 = (f32[8,384]{1,0:T(8,128)S(1)}, f32[8,384]{1,0:T(8,128)S(1)}, u32[]{:S(2)}, u32[]{:S(2)}) collective-permute-start(f32[8,384]{1,0:T(8,128)S(1)} %get-tuple-element.44), channel_id=1, source_target_pairs={{0,128},{128,0},{1,129},{129,1},{2,130},{130,2},{3,131},{131,3},{4... | collective-permute-start | bytes 36872 | tf_op jit(solution)/shard_map/ppermute | solution.py:237
  110.4 4.1 %collective-permute-start.27 = (f32[8,384]{1,0:T(8,128)S(1)}, f32[8,384]{1,0:T(8,128)S(1)}, u32[]{:S(2)}, u32[]{:S(2)}) collective-permute-start(f32[8,384]{1,0:T(8,128)S(1)} %get-tuple-element.44), channel_id=1, source_target_pairs={{0,132},{132,0},{4,128},{128,4},{1,133},{133,1},{5,129},{129,5},{2... | collective-permute-start | bytes 36872 | tf_op jit(solution)/shard_map/ppermute | solution.py:265

commit v2 on v1

v2 whole, which is shorter than its diff:
```python
import functools
import math

import jax
import jax.numpy as jnp
from jax import lax
from jax.experimental import pallas as pl
from jax.experimental.pallas import tpu as pltpu
from jax.sharding import Mesh
from jax.sharding import PartitionSpec as P

HEADS = 16
DH = 128
SCALE = 1.0 / math.sqrt(DH)
LOG2E = math.log2(math.e)
LIMIT = 2.0**40
F32 = jnp.float32
BF16 = jnp.bfloat16
SWAP = ((0, 1), (1, 0))
PARAMS = pltpu.CompilerParams(vmem_limit_bytes=60 << 20)


def nt(a, b):
    return lax.dot_general(a, b, (((1,), (1,)), ((), ())), preferred_element_type=F32)


def nn(a, b):
    return lax.dot_general(a, b, (((1,), (0,)), ((), ())), preferred_element_type=F32)


def pack_kernel(q, k, v, qt, kt, vt, own, other, sems):
    rows = q.shape[0]
    half = rows // 2
    yh = lax.axis_index("yh")
    copies = []
    for which, out in enumerate((own, other)):
        head = yh if which == 0 else 1 - yh
        cols = pl.ds(pl.multiple_of(head * DH, DH), DH)
        for at, ref in enumerate((kt, k, v, vt)):
            copies.append((ref.at[:, cols], out.at[0:rows, at * DH : (at + 1) * DH]))
        for at, ref in enumerate((q, qt, q, qt)):
            part = slice(0, half) if at < 2 else slice(half, rows)
            copies.append((ref.at[part, cols], out.at[rows : rows + half, at * DH : (at + 1) * DH]))
    copies = [pltpu.make_async_copy(a, b, sems.at[i]) for i, (a, b) in enumerate(copies)]
    for copy in copies:
        copy.start()
    for copy in copies:
        copy.wait()


def pack(*arrays):
    rows = arrays[0].shape[0]
    out = jax.ShapeDtypeStruct((rows + rows // 2, 4 * DH), BF16)
    return pl.pallas_call(
        pack_kernel,
        out_shape=(out, out),
        in_specs=[pl.BlockSpec(memory_space=pl.ANY)] * 6,
        out_specs=[pl.BlockSpec(memory_space=pl.ANY)] * 2,
        scratch_shapes=[pltpu.SemaphoreType.DMA((16,))],
        compiler_params=PARAMS,
        cost_estimate=pl.CostEstimate(flops=0, bytes_accessed=12 * rows * 2 * DH * 2, transcendentals=0),
        name="pack",
    )(*arrays)


def lanes(x):
    out = x[:, :DH]
    for i in range(1, x.shape[1] // DH):
        out = out + x[:, i * DH : (i + 1) * DH]
    return out


def wide(x, times):
    return jnp.concatenate([x] * times, axis=1)


def part(query, kv, state, exact):
    keys = kv.shape[0]
    scores = nt(query[:, :DH], kv[:, DH : 2 * DH]) * (SCALE * LOG2E)
    tangent = nt(query, kv[:, : 2 * DH])
    old = state
    if exact:
        top = jnp.broadcast_to(jnp.max(scores, axis=1, keepdims=True), (query.shape[0], DH))
        if old is not None:
            top = jnp.maximum(top, old[4])
    else:
        top = old[4]
    weights = jnp.exp2(scores - wide(top, keys // DH))
    tilted = weights * tangent
    total, cross = lanes(weights), lanes(tilted)
    both = nn(weights.astype(BF16), kv[:, 2 * DH :])
    moved = both[:, DH:] + nn(tilted.astype(BF16), kv[:, 2 * DH : 3 * DH]) * SCALE
    new = (both[:, :DH], moved, total, cross)
    if old is None:
        return (*new, top)
    if exact:
        factor = jnp.exp2(old[4] - top)
        return (*(n + o * factor for n, o in zip(new, old[:4])), top)
    return (*(n + o for n, o in zip(new, old[:4])), top)


def read(ref, rows=slice(None)):
    return tuple(ref[rows, i * DH : (i + 1) * DH] for i in range(5))


def write(ref, state, rows=slice(None)):
    for i, piece in enumerate(state):
        ref[rows, i * DH : (i + 1) * DH] = piece


def attend_kernel(blocks, first, last, *refs):
    q_ref = refs[0]
    kv_refs = refs[1 : 1 + blocks]
    at = 1 + blocks
    if not first:
        old_ref = refs[at]
        at += 1
    outs = refs[at : at + (2 if last else 1)]
    kv = refs[at + len(outs)]
    new_ref = refs[-1] if last else outs[0]

    @pl.when(pl.program_id(0) == 0)
    def _():
        at = 0
        for ref in kv_refs:
            kv[at : at + ref.shape[0], :] = ref[...]
            at += ref.shape[0]

    if first:
        write(new_ref, part(q_ref[...], kv, None, True))
    else:
        state = part(q_ref[...], kv, read(old_ref), False)
        write(new_ref, state)
        fine = jnp.max(state[2]) < LIMIT

        @pl.when(jnp.logical_not(fine))
        def _():
            def body(i, carry):
                rows = pl.ds(pl.multiple_of(i * 64, 64), 64)
                write(new_ref, part(q_ref[rows, :], kv, read(old_ref, rows), True), rows)
                return carry

            lax.fori_loop(0, q_ref.shape[0] // 64, body, 0)

    if last:
        out, stats = outs
        primal, moved, total, cross, top = read(new_ref)
        total = jnp.sum(total, axis=1, keepdims=True)
        cross = jnp.sum(cross, axis=1, keepdims=True)
        inverse = 1.0 / total
        out[:, :DH] = (primal * inverse).astype(out.dtype)
        out[:, DH:] = (moved * inverse).astype(out.dtype)
        lane = lax.broadcasted_iota(jnp.int32, top.shape, 1)
        stats[...] = jnp.where(lane == 0, top + jnp.log2(total), cross * (SCALE * inverse))


def attend(query, kvs, state, span=None, kind=None, tile=256):
    begin, end = span or (0, query.shape[0])
    rows = end - begin
    tiles, off = rows // tile, begin // tile
    height = lambda kv: 384 if kv.shape[0] == 576 else kv.shape[0]
    keys = sum(height(kv) for kv in kvs)
    block = lambda width, base: pl.BlockSpec((tile, width), lambda i: (i + base, 0))
    whole = lambda a: pl.BlockSpec((height(a), 4 * DH), lambda i: (0, 0), pipeline_mode=pl.Buffered(1))
    ins = [query, *kvs]
    in_specs = [block(2 * DH, off)] + [whole(kv) for kv in kvs]
    if state is not None:
        ins.append(state)
        in_specs.append(block(5 * DH, off))
    scratch = [pltpu.VMEM((keys, 4 * DH), BF16)]
    if kind is None:
        out_specs = [block(5 * DH, 0)]
        shapes = [jax.ShapeDtypeStruct((rows, 5 * DH), F32)]
    else:
        out_specs = [block(2 * DH, 0), block(DH, 0)]
        shapes = [jax.ShapeDtypeStruct((rows, 2 * DH), kind), jax.ShapeDtypeStruct((rows, DH), F32)]
        scratch.append(pltpu.VMEM((tile, 5 * DH), F32))
    out = pl.pallas_call(
        functools.partial(attend_kernel, len(kvs), state is None, kind is not None),
        grid=(tiles,),
        in_specs=in_specs,
        out_specs=out_specs,
        out_shape=shapes,
        scratch_shapes=scratch,
        compiler_params=PARAMS,
        cost_estimate=pl.CostEstimate(
            flops=2 * 8 * rows * keys * DH,
            bytes_accessed=keys * 4 * DH * 2 + rows * 5 * DH * 8,
            transcendentals=rows * keys,
        ),
        name="attend",
    )(*ins)
    return out if kind is not None else out[0]


def join_kernel(mine, mine_stat, other, other_stat, keep, send, squares):
    step = pl.program_id(0)
    yh = lax.axis_index("yh")
    top_a, top_b = mine_stat[:, 0:1], other_stat[:, 0:1]
    top = jnp.maximum(top_a, top_b)
    part_a, part_b = jnp.exp2(top_a - top), jnp.exp2(top_b - top)
    inverse = 1.0 / (part_a + part_b)
    part_a, part_b = part_a * inverse, part_b * inverse
    both = mine[...] * part_a + other[...].astype(F32) * part_b
    cross = mine_stat[:, 1:2] * part_a + other_stat[:, 1:2] * part_b
    out = both[:, :DH]
    moved = both[:, DH:] - cross * out

    @pl.when(step == 0)
    def _():
        keep[:, :DH] = out
        keep[:, DH:] = moved

    @pl.when(step == 1)
    def _():
        send[:, :DH] = out.astype(BF16)
        send[:, DH:] = moved.astype(BF16)

    owner = jnp.where(step == 0, yh, 1 - yh)
    squares[pl.ds(pl.multiple_of(owner * 8, 8), 8), :] = lax.dot_general(
        jnp.ones((8, DH), F32),
        moved * moved,
        (((1,), (1,)), ((), ())),
        precision=lax.Precision.HIGHEST,
        preferred_element_type=F32,
    )


def join(mine, mine_stat, other, other_stat):
    half = mine.shape[0] // 2
    row = lambda width: pl.BlockSpec((half, width), lambda i: (i, 0))
    fixed = lambda *shape: pl.BlockSpec(shape, lambda i: (0, 0))
    return pl.pallas_call(
        join_kernel,
        grid=(2,),
        in_specs=[row(2 * DH), row(DH), row(2 * DH), row(DH)],
        out_specs=[fixed(half, 2 * DH), fixed(half, 2 * DH), fixed(16, half)],
        out_shape=[
            jax.ShapeDtypeStruct((half, 2 * DH), F32),
            jax.ShapeDtypeStruct((half, 2 * DH), BF16),
            jax.ShapeDtypeStruct((16, half), F32),
        ],
        compiler_params=PARAMS,
        name="join",
    )(mine, mine_stat, other, other_stat)


def finish_kernel(keep, come, squares, attended, unit):
    flip = lax.axis_index("yh") == 1
    mean = lax.dot_general(
        squares[...],
        jnp.full((16, DH), 1.0 / (HEADS * DH), F32),
        (((0,), (0,)), ((), ())),
        precision=lax.Precision.HIGHEST,
        preferred_element_type=F32,
    )
    inverse = 1.0 / jnp.sqrt(mean + 1e-06)
    mine, other = keep[:, :DH].astype(BF16), come[:, :DH]
    attended[:, :DH] = jnp.where(flip, other, mine)
    attended[:, DH:] = jnp.where(flip, mine, other)
    mine = (keep[:, DH:] * inverse).astype(BF16)
    other = (come[:, DH:].astype(F32) * inverse).astype(BF16)
    unit[:, :DH] = jnp.where(flip, other, mine)
    unit[:, DH:] = jnp.where(flip, mine, other)


def finish(*arrays):
    out = jax.ShapeDtypeStruct(arrays[1].shape, BF16)
    return pl.pallas_call(finish_kernel, out_shape=(out, out), compiler_params=PARAMS, name="finish")(*arrays)


def on_device(ring, q, k, v, qt, kt, vt):
    tokens = q.shape[0]
    hop_pairs = [(z * 2 + c, (z + 1 - 2 * c) % ring * 2 + c) for z in range(ring) for c in range(2)]
    hop = lambda a: lax.ppermute(a, ("z", "core"), hop_pairs)
    over_y = lambda a: lax.ppermute(a, "yh", SWAP)
    over_core = lambda a: lax.ppermute(a, "core", SWAP)
    queries = lambda a: (a[tokens:, : 2 * DH], a[tokens:, 2 * DH :])

    own, other = pack(q, k, v, qt, kt, vt)
    peer = over_y(other)
    own_core, peer_core = over_core(own), over_core(peer)
    near_x = jnp.concatenate([own[:tokens], own_core[:tokens]], axis=0)
    far_x = jnp.concatenate([peer[:tokens], peer_core[:tokens]], axis=0)
    query = jnp.concatenate([piece for a in (own, peer, own_core, peer_core) for piece in queries(a)], axis=0)

    near_hops, far_hops = [], []
    for _ in range(ring // 2 - 1):
        near_x, far_x = hop(near_x), hop(far_x)
        near_hops.append(near_x)
        far_hops.append(far_x)
    near_hops.append(hop(near_x[:tokens]))
    far_hops.append(hop(far_x[:tokens]))

    state = attend(query, [own, peer, near_hops[0]], None)
    state = attend(query, [near_hops[1], far_hops[0]], state)
    state = attend(query, [near_hops[2], far_hops[1]], state)
    state = attend(query, [far_hops[2]], state)
    ends = [near_hops[3], far_hops[3]]
    rows = query.shape[0]
    far, far_stat = attend(query, ends, state, (rows // 2, rows), BF16)
    other, other_stat = over_core(far), over_core(far_stat)
    near, near_stat = attend(query, ends, state, (0, rows // 2), F32)
    keep, send, squares = join(near, near_stat, other, other_stat)
    come = over_y(send)
    squares = lax.all_to_all(squares, ("yh", "yl", "x"), 0, 0, tiled=True)
    return finish(keep, come, squares)


def solution(mesh):
    fine = Mesh(mesh.devices.reshape(2, -1, 2, 2, mesh.shape["head"] // 2), ("yh", "z", "core", "yl", "x"))
    spec = P(("yh", "z", "core"), ("yl", "x"))
    return jax.shard_map(
        functools.partial(on_device, fine.shape["z"]),
        mesh=fine,
        in_specs=(spec,) * 6,
        out_specs=(spec, spec),
        check_vma=False,
    )
```

time: 117 us -> 175 us (1.50)
  Pallas kernels: 41.3 us -> 89.1 us
  starting transfers between devices: 43.3 us -> 30.3 us
  waiting for transfers between devices: 21 us -> 33.4 us
  blocking collectives: 0 us -> 10.9 us
  local copies, waits for them, and re-layouts: 9.18 us -> 7.41 us
    pallas_call x2, Pallas kernels: 1.43 us -> 39.3 us  [the longest x1 37 us: pack(): pl.pallas_call(pack_kernel, out_shape=(out, out), in_specs=[pl.BlockSpec(...]
    all_to_all x0 -> x1, blocking collectives: none -> 10.9 us  [on_device(): squares = lax.all_to_all(squares, ('yh', 'yl', 'x'), 0, 0, tiled=True)]
    ppermute x19 -> x8, starting transfers between devices: 28.4 us -> 19.9 us  [on_device(): hop = lambda a: lax.ppermute(a, ('z', 'core'), hop_pairs)]
    ppermute x19 -> x8, waiting for transfers between devices: 13.6 us -> 22 us  [on_device(): hop = lambda a: lax.ppermute(a, ('z', 'core'), hop_pairs)]
    pallas_call x5 -> x6, Pallas kernels: 38.6 us -> 46.5 us  [attend(): pl.pallas_call(functools.partial(attend_kernel, len(kvs), state is None,...]
    ppermute x5 -> x2, waiting for transfers between devices: 5.6 us -> 11.4 us  [on_device(): over_y = lambda a: lax.ppermute(a, 'yh', SWAP)]
    unnamed x21 -> x32, local copies, waits for them, and re-layouts: 9.12 us -> 5.48 us
    ppermute x5 -> x2, starting transfers between devices: 9.9 us -> 6.76 us  [on_device(): over_y = lambda a: lax.ppermute(a, 'yh', SWAP)]
  transfers between devices with their start and end apart: 28 -> 14, of which waited for: 9 -> 5; matrix products, arithmetic and copies ran while one was open for 0% -> 3% of each run, Pallas kernels for 28% -> 24%
where the time goes in v2:
time: 175 us; the launch traced here: 172 us
  Pallas kernels  89.1 us (51%)
  waiting for transfers between devices  33.4 us (19%)
  starting transfers between devices  30.3 us (17%)
  blocking collectives  10.9 us (6%)
  local copies, waits for them, and re-layouts  7.41 us (4%)
    pallas_call x6, Pallas kernels, attend(): pl.pallas_call(functools.partial(attend_kernel, len(kvs), state is None,...  46.5 us
    pallas_call x1, Pallas kernels, pack(): pl.pallas_call(pack_kernel, out_shape=(out, out), in_specs=[pl.BlockSpec(...  37 us
    ppermute x8, waiting for transfers between devices, on_device(): hop = lambda a: lax.ppermute(a, ('z', 'core'), hop_pairs)  22 us
    ppermute x8, starting transfers between devices, on_device(): hop = lambda a: lax.ppermute(a, ('z', 'core'), hop_pairs)  19.9 us
    ppermute x2, waiting for transfers between devices, on_device(): over_y = lambda a: lax.ppermute(a, 'yh', SWAP)  11.4 us
    all_to_all x1, blocking collectives, on_device(): squares = lax.all_to_all(squares, ('yh', 'yl', 'x'), 0, 0, tiled=True)  10.9 us
    ppermute x2, starting transfers between devices, on_device(): over_y = lambda a: lax.ppermute(a, 'yh', SWAP)  6.76 us
    unnamed x32, local copies, waits for them, and re-layouts  5.48 us
  transfers between devices with their start and end apart: 14, of which 5 were waited for; matrix products, arithmetic and copies ran while one was open for 3% of the time, Pallas kernels for 24%

profile of v2, /device:TPU:1, one launch (start us, length us, event | category | flops | bytes accessed | tf_op | source)
XLA Modules:
  0.0 172.0 jit_solution(3751014313040001002)
XLA Ops:
  0.6 37.0 %pack.1 = (bf16[576,512]{1,0:T(8,128)(2,1)}, bf16[576,512]{1,0:T(8,128)(2,1)}) custom-call(bf16[384,256]{1,0:T(8,128)(2,1)} %q.1, bf16[384,256]{1,0:T(8,128)(2,1)} %k.1, bf16[384,256]{1,0:T(8,128)(2,1)} %v.1, bf16[384,256]{1,0:T(8,128)(2,1)} %qt.1, bf16[384,256]{1,0:T(8,128)(2,1)} %kt.1, bf16[384,256]{1,0:T(8,128)(2,1)} %vt.1), custom_call_target="tpu_custom_call" | custom-call | bytes 2359296 | tf_op jit(solution)/shard_map/pack/pallas_call | solution.py:54
  37.6 3.8 %collective-permute-start = (bf16[576,512]{1,0:T(8,128)(2,1)}, bf16[576,512]{1,0:T(8,128)(2,1)S(1)}, u32[]{:S(2)}, u32[]{:S(2)}) collective-permute-start(bf16[576,512]{1,0:T(8,128)(2,1)} %get-tuple-element.12), channel_id=1, source_target_pairs={{0,128},{128,0},{1,129},{129,1},{2,130},{130,2},{3,131},{131,3},{4... | collective-permute-start | bytes 1769480 | tf_op jit(solution)/shard_map/ppermute | solution.py:276
  41.5 1.0 collective-permute-start.1
  42.4 11.4 %collective-permute-done.refs_2_ = bf16[576,512]{1,0:T(8,128)(2,1)S(1)} collective-permute-done((bf16[576,512]{1,0:T(8,128)(2,1)}, bf16[576,512]{1,0:T(8,128)(2,1)S(1)}, u32[]{:S(2)}, u32[]{:S(2)}) %collective-permute-start) | collective-permute-done | bytes 589856 | tf_op jit(solution)/shard_map/ppermute | solution.py:276
  53.8 0.0 copy-start.4
  53.8 2.2 %collective-permute-start.2 = (bf16[576,512]{1,0:T(8,128)(2,1)S(1)}, bf16[576,512]{1,0:T(8,128)(2,1)S(1)}, u32[]{:S(2)}, u32[]{:S(2)}) collective-permute-start(bf16[576,512]{1,0:T(8,128)(2,1)S(1)} %collective-permute-done.refs_2_), channel_id=1, source_target_pairs={{0,8},{8,0},{1,9},{9,1},{2,10},{10,2},{3,11},{11,3},{4,12},{12,4},... | collective-permute-start | bytes 1769480 | tf_op jit(solution)/shard_map/ppermute | solution.py:277
  56.0 1.0 slice.50
  57.0 0.0 collective-permute-done.1
  57.0 0.1 pad_maximum_fusion
  57.1 5.7 %collective-permute-start.3 = (bf16[768,512]{1,0:T(8,128)(2,1)S(1)}, bf16[768,512]{1,0:T(8,128)(2,1)S(1)}, u32[]{:S(2)}, u32[]{:S(2)}) collective-permute-start(bf16[768,512]{1,0:T(8,128)(2,1)S(1)} %pad_maximum_fusion), channel_id=1, source_target_pairs={{0,16},{8,120},{16,32},{24,8},{32,48},{40,24},{48,64},{56,40},{64,... | collective-permute-start | bytes 2359304 | tf_op jit(solution)/shard_map/ppermute | solution.py:275
  62.8 0.0 collective-permute-done.2
  62.9 0.1 pad_maximum_fusion.1
  62.9 0.8 collective-permute-start.7
  63.7 0.9 slice_dynamic-update-slice_fusion.7
  64.6 0.9 slice_dynamic-update-slice_fusion.6
  65.5 0.0 copy-done.4
  65.6 6.2 %collective-permute-done.3.refs_3_ = bf16[768,512]{1,0:T(8,128)(2,1)S(1)} collective-permute-done((bf16[768,512]{1,0:T(8,128)(2,1)S(1)}, bf16[768,512]{1,0:T(8,128)(2,1)S(1)}, u32[]{:S(2)}, u32[]{:S(2)}) %collective-permute-start.3) | collective-permute-done | bytes 786464 | tf_op jit(solution)/shard_map/ppermute | solution.py:275
  71.7 3.1 %collective-permute-start.4 = (bf16[768,512]{1,0:T(8,128)(2,1)S(1)}, bf16[768,512]{1,0:T(8,128)(2,1)S(1)}, u32[]{:S(2)}, u32[]{:S(2)}) collective-permute-start(bf16[768,512]{1,0:T(8,128)(2,1)S(1)} %collective-permute-done.3.refs_3_), channel_id=1, source_target_pairs={{0,16},{8,120},{16,32},{24,8},{32,48},{40,24},{48,64},{56,40},{64,... | collective-permute-start | bytes 2359304 | tf_op jit(solution)/shard_map/ppermute | solution.py:275
  74.8 5.3 %collective-permute-done.7.refs_2_ = bf16[768,512]{1,0:T(8,128)(2,1)S(1)} collective-permute-done((bf16[768,512]{1,0:T(8,128)(2,1)S(1)}, bf16[768,512]{1,0:T(8,128)(2,1)S(1)}, u32[]{:S(2)}, u32[]{:S(2)}) %collective-permute-start.7) | collective-permute-done | bytes 786464 | tf_op jit(solution)/shard_map/ppermute | solution.py:275
  80.2 0.0 copy-start.10
  80.2 3.1 %collective-permute-start.8 = (bf16[768,512]{1,0:T(8,128)(2,1)S(1)}, bf16[768,512]{1,0:T(8,128)(2,1)}, u32[]{:S(2)}, u32[]{:S(2)}) collective-permute-start(bf16[768,512]{1,0:T(8,128)(2,1)S(1)} %collective-permute-done.7.refs_2_), channel_id=1, source_target_pairs={{0,16},{8,120},{16,32},{24,8},{32,48},{40,24},{48,64},{56,40},{64,... | collective-permute-start | bytes 2359304 | tf_op jit(solution)/shard_map/ppermute | solution.py:275
  83.3 0.0 copy-start
  83.3 5.2 %collective-permute-done.4.refs_1_ = bf16[768,512]{1,0:T(8,128)(2,1)S(1)} collective-permute-done((bf16[768,512]{1,0:T(8,128)(2,1)S(1)}, bf16[768,512]{1,0:T(8,128)(2,1)S(1)}, u32[]{:S(2)}, u32[]{:S(2)}) %collective-permute-start.4) | collective-permute-done | bytes 786464 | tf_op jit(solution)/shard_map/ppermute | solution.py:275
  88.6 0.0 copy-start.11
  88.6 3.1 %collective-permute-start.5 = (bf16[768,512]{1,0:T(8,128)(2,1)S(1)}, bf16[768,512]{1,0:T(8,128)(2,1)S(1)}, u32[]{:S(2)}, u32[]{:S(2)}) collective-permute-start(bf16[768,512]{1,0:T(8,128)(2,1)S(1)} %collective-permute-done.4.refs_1_), channel_id=1, source_target_pairs={{0,16},{8,120},{16,32},{24,8},{32,48},{40,24},{48,64},{56,40},{64,... | collective-permute-start | bytes 2359304 | tf_op jit(solution)/shard_map/ppermute | solution.py:275
  91.7 0.0 copy-done.10
  91.7 5.3 %collective-permute-done.8.refs_2_ = bf16[768,512]{1,0:T(8,128)(2,1)} collective-permute-done((bf16[768,512]{1,0:T(8,128)(2,1)S(1)}, bf16[768,512]{1,0:T(8,128)(2,1)}, u32[]{:S(2)}, u32[]{:S(2)}) %collective-permute-start.8) | collective-permute-done | bytes 786464 | tf_op jit(solution)/shard_map/ppermute | solution.py:275
  97.0 3.2 %collective-permute-start.9 = (bf16[768,512]{1,0:T(8,128)(2,1)}, bf16[768,512]{1,0:T(8,128)(2,1)S(1)}, u32[]{:S(2)}, u32[]{:S(2)}) collective-permute-start(bf16[768,512]{1,0:T(8,128)(2,1)} %collective-permute-done.8.refs_2_), channel_id=1, source_target_pairs={{0,16},{8,120},{16,32},{24,8},{32,48},{40,24},{48,64},{56,40},{64,... | collective-permute-start | bytes 2359304 | tf_op jit(solution)/shard_map/ppermute | solution.py:275
  100.2 0.0 copy-done.9
  100.2 0.0 copy-done
  100.2 9.9 %attend.6.refs_3_ = f32[1536,640]{1,0:T(8,128)} custom-call(bf16[1536,256]{1,0:T(8,128)(2,1)} %copy-done, bf16[576,512]{1,0:T(8,128)(2,1)} %get-tuple-element.11.refs_1_, bf16[576,512]{1,0:T(8,128)(2,1)} %copy-done.4, bf16[768,512]{1,0:T(8,128)(2,1)} %copy-done.9), custom_call_target="tpu_custom_call" | custom-call | flops 4831838208 | bytes 9437184 | tf_op jit(solution)/shard_map/attend/pallas_call | solution.py:178
  110.2 0.0 copy-done.11
  110.2 9.6 %attend.7.refs_3_ = f32[1536,640]{1,0:T(8,128)} custom-call(bf16[1536,256]{1,0:T(8,128)(2,1)} %copy-done, bf16[768,512]{1,0:T(8,128)(2,1)} %copy-done.11, bf16[768,512]{1,0:T(8,128)(2,1)} %copy-done.10, f32[1536,640]{1,0:T(8,128)} %attend.6.refs_3_), custom_call_target="tpu_custom_call" | custom-call | flops 4831838208 | bytes 9437184 | tf_op jit(solution)/shard_map/attend/pallas_call | solution.py:178
  119.7 0.0 collective-permute-done.5.refs_1_
  119.7 0.0 copy-start.7
  119.8 0.1 collective-permute-start.6
  119.9 0.0 collective-permute-done.9.refs_1_
  119.9 0.0 copy-start.1
  119.9 0.8 collective-permute-start.10
  120.7 0.0 copy-done.7
  120.7 9.6 %attend.8.refs_2_ = f32[1536,640]{1,0:T(8,128)} custom-call(bf16[1536,256]{1,0:T(8,128)(2,1)} %copy-done, bf16[768,512]{1,0:T(8,128)(2,1)} %copy-done.7, bf16[768,512]{1,0:T(8,128)(2,1)} %collective-permute-done.8.refs_2_, f32[1536,640]{1,0:T(8,128)} %attend.7.refs_3_), custom_call_target="tpu_custom_call" | custom-call | flops 4831838208 | bytes 9437184 | tf_op jit(solution)/shard_map/attend/pallas_call | solution.py:178
  130.3 0.0 copy-done.1
  130.3 7.6 %attend.9.refs_3_ = f32[1536,640]{1,0:T(8,128)} custom-call(bf16[1536,256]{1,0:T(8,128)(2,1)} %copy-done, bf16[768,512]{1,0:T(8,128)(2,1)} %copy-done.1, f32[1536,640]{1,0:T(8,128)} %attend.8.refs_2_), custom_call_target="tpu_custom_call" | custom-call | flops 2415919104 | bytes 8650752 | tf_op jit(solution)/shard_map/attend/pallas_call | solution.py:178
  137.9 0.0 collective-permute-done.6.refs_1_
  137.9 0.0 collective-permute-done.10.refs_2_
  137.9 0.7 copy-done.2
  138.6 0.7 copy-done.3
  139.4 4.9 %attend.11 = (bf16[768,256]{1,0:T(8,128)(2,1)}, f32[768,128]{1,0:T(8,128)}) custom-call(bf16[1536,256]{1,0:T(8,128)(2,1)} %copy-done, bf16[384,512]{1,0:T(8,128)(2,1)} %copy-done.2, bf16[384,512]{1,0:T(8,128)(2,1)} %copy-done.3, f32[1536,640]{1,0:T(8,128)} %attend.9.refs_3_), custom_call_target="tpu_custom_call" | custom-call | flops 1207959552 | bytes 4718592 | tf_op jit(solution)/shard_map/attend/pallas_call | solution.py:178
  144.2 0.3 collective-permute-start.11
  144.6 0.2 collective-permute-start.12
  144.7 5.0 %attend.10 = (f32[768,256]{1,0:T(8,128)}, f32[768,128]{1,0:T(8,128)}) custom-call(bf16[1536,256]{1,0:T(8,128)(2,1)} %copy-done, bf16[384,512]{1,0:T(8,128)(2,1)} %copy-done.2, bf16[384,512]{1,0:T(8,128)(2,1)} %copy-done.3, f32[1536,640]{1,0:T(8,128)} %attend.9.refs_3_), custom_call_target="tpu_custom_call" | custom-call | flops 1207959552 | bytes 4718592 | tf_op jit(solution)/shard_map/attend/pallas_call | solution.py:178
  149.7 0.0 collective-permute-done.11.other
  149.7 0.0 collective-permute-done.12.other_stat
  149.7 0.0 copy-start.6
  149.7 0.7 copy-done.5
  150.4 0.1 copy-done.6
  150.6 3.3 %join.1 = (f32[384,256]{1,0:T(8,128)}, bf16[384,256]{1,0:T(8,128)(2,1)}, f32[16,384]{1,0:T(8,128)}) custom-call(f32[768,256]{1,0:T(8,128)} %get-tuple-element.13.mine, f32[768,128]{1,0:T(8,128)} %get-tuple-element.14.mine_stat, bf16[768,256]{1,0:T(8,128)(2,1)} %copy-done.5, f32[768,128]{1,0:T(8,128)} %copy-done.6), custom_call_target="tpu_custom_call" | custom-call | tf_op jit(solution)/shard_map/join/pallas_call | solution.py:233
  153.9 2.9 %collective-permute-start.13 = (bf16[384,256]{1,0:T(8,128)(2,1)}, bf16[384,256]{1,0:T(8,128)(2,1)S(1)}, u32[]{:S(2)}, u32[]{:S(2)}) collective-permute-start(bf16[384,256]{1,0:T(8,128)(2,1)} %get-tuple-element.18), channel_id=1, source_target_pairs={{0,128},{128,0},{1,129},{129,1},{2,130},{130,2},{3,131},{131,3},{4... | collective-permute-start | bytes 589832 | tf_op jit(solution)/shard_map/ppermute | solution.py:276
  156.8 0.8 copy.8
  157.6 10.9 %all_to_all.11 = f32[16,1,384]{2,1,0:T(1,128)S(1)} all-to-all(f32[16,1,384]{2,1,0:T(1,128)S(1)} %copy.8), channel_id=1, replica_groups=mesh['yh'=2,'z'=8,'core'=2,'yl'=2,'x'=4] {'yh','yl','x'}, dimensions={0} | all-to-all | bytes 49152 | tf_op jit(solution)/shard_map/all_to_all | solution.py:306
  168.4 0.6 copy.11
  169.0 0.0 collective-permute-done.13.come
  169.1 0.7 copy-done.8
  169.7 2.3 %finish.1 = (bf16[384,256]{1,0:T(8,128)(2,1)}, bf16[384,256]{1,0:T(8,128)(2,1)}) custom-call(f32[384,256]{1,0:T(8,128)} %get-tuple-element.17.keep, bf16[384,256]{1,0:T(8,128)(2,1)} %copy-done.8, f32[16,384]{1,0:T(8,128)} %bitcast.4), custom_call_target="tpu_custom_call" | custom-call | tf_op jit(solution)/shard_map/finish/pallas_call | solution.py:269
  (16 shorter events, 0.2 us)
Async XLA Ops:
  37.6 16.1 %collective-permute-start = (bf16[576,512]{1,0:T(8,128)(2,1)}, bf16[576,512]{1,0:T(8,128)(2,1)S(1)}, u32[]{:S(2)}, u32[]{:S(2)}) collective-permute-start(bf16[576,512]{1,0:T(8,128)(2,1)} %get-tuple-element.12), channel_id=1, source_target_pairs={{0,128},{128,0},{1,129},{129,1},{2,130},{130,2},{3,131},{131,3},{4... | collective-permute-start | bytes 1769480 | tf_op jit(solution)/shard_map/ppermute | solution.py:276
  41.5 15.5 %collective-permute-start.1 = (bf16[576,512]{1,0:T(8,128)(2,1)}, bf16[576,512]{1,0:T(8,128)(2,1)S(1)}, u32[]{:S(2)}, u32[]{:S(2)}) collective-permute-start(bf16[576,512]{1,0:T(8,128)(2,1)} %get-tuple-element.11.refs_1_), channel_id=1, source_target_pairs={{0,8},{8,0},{1,9},{9,1},{2,10},{10,2},{3,11},{11,3},{4,12},{12,4},... | collective-permute-start | bytes 1769480 | tf_op jit(solution)/shard_map/ppermute | solution.py:277
  53.8 11.8 %copy-start.4 = (bf16[576,512]{1,0:T(8,128)(2,1)}, bf16[576,512]{1,0:T(8,128)(2,1)S(1)}, u32[]{:S(2)}) copy-start(bf16[576,512]{1,0:T(8,128)(2,1)S(1)} %collective-permute-done.refs_2_) | copy-start | bytes 1769476
  53.8 9.0 %collective-permute-start.2 = (bf16[576,512]{1,0:T(8,128)(2,1)S(1)}, bf16[576,512]{1,0:T(8,128)(2,1)S(1)}, u32[]{:S(2)}, u32[]{:S(2)}) collective-permute-start(bf16[576,512]{1,0:T(8,128)(2,1)S(1)} %collective-permute-done.refs_2_), channel_id=1, source_target_pairs={{0,8},{8,0},{1,9},{9,1},{2,10},{10,2},{3,11},{11,3},{4,12},{12,4},... | collective-permute-start | bytes 1769480 | tf_op jit(solution)/shard_map/ppermute | solution.py:277
  57.1 14.6 %collective-permute-start.3 = (bf16[768,512]{1,0:T(8,128)(2,1)S(1)}, bf16[768,512]{1,0:T(8,128)(2,1)S(1)}, u32[]{:S(2)}, u32[]{:S(2)}) collective-permute-start(bf16[768,512]{1,0:T(8,128)(2,1)S(1)} %pad_maximum_fusion), channel_id=1, source_target_pairs={{0,16},{8,120},{16,32},{24,8},{32,48},{40,24},{48,64},{56,40},{64,... | collective-permute-start | bytes 2359304 | tf_op jit(solution)/shard_map/ppermute | solution.py:275
  62.9 17.2 %collective-permute-start.7 = (bf16[768,512]{1,0:T(8,128)(2,1)S(1)}, bf16[768,512]{1,0:T(8,128)(2,1)S(1)}, u32[]{:S(2)}, u32[]{:S(2)}) collective-permute-start(bf16[768,512]{1,0:T(8,128)(2,1)S(1)} %pad_maximum_fusion.1), channel_id=1, source_target_pairs={{0,16},{8,120},{16,32},{24,8},{32,48},{40,24},{48,64},{56,40},{64,... | collective-permute-start | bytes 2359304 | tf_op jit(solution)/shard_map/ppermute | solution.py:275
  71.7 28.5 %copy-start.9 = (bf16[768,512]{1,0:T(8,128)(2,1)}, bf16[768,512]{1,0:T(8,128)(2,1)S(1)}, u32[]{:S(2)}) copy-start(bf16[768,512]{1,0:T(8,128)(2,1)S(1)} %collective-permute-done.3.refs_3_) | copy-start | bytes 2359300
  71.7 16.9 %collective-permute-start.4 = (bf16[768,512]{1,0:T(8,128)(2,1)S(1)}, bf16[768,512]{1,0:T(8,128)(2,1)S(1)}, u32[]{:S(2)}, u32[]{:S(2)}) collective-permute-start(bf16[768,512]{1,0:T(8,128)(2,1)S(1)} %collective-permute-done.3.refs_3_), channel_id=1, source_target_pairs={{0,16},{8,120},{16,32},{24,8},{32,48},{40,24},{48,64},{56,40},{64,... | collective-permute-start | bytes 2359304 | tf_op jit(solution)/shard_map/ppermute | solution.py:275
  80.2 11.5 %copy-start.10 = (bf16[768,512]{1,0:T(8,128)(2,1)}, bf16[768,512]{1,0:T(8,128)(2,1)S(1)}, u32[]{:S(2)}) copy-start(bf16[768,512]{1,0:T(8,128)(2,1)S(1)} %collective-permute-done.7.refs_2_) | copy-start | bytes 2359300
  80.2 16.9 %collective-permute-start.8 = (bf16[768,512]{1,0:T(8,128)(2,1)S(1)}, bf16[768,512]{1,0:T(8,128)(2,1)}, u32[]{:S(2)}, u32[]{:S(2)}) collective-permute-start(bf16[768,512]{1,0:T(8,128)(2,1)S(1)} %collective-permute-done.7.refs_2_), channel_id=1, source_target_pairs={{0,16},{8,120},{16,32},{24,8},{32,48},{40,24},{48,64},{56,40},{64,... | collective-permute-start | bytes 2359304 | tf_op jit(solution)/shard_map/ppermute | solution.py:275
  83.3 16.9 %copy-start = (bf16[1536,256]{1,0:T(8,128)(2,1)}, bf16[1536,256]{1,0:T(8,128)(2,1)S(1)}, u32[]{:S(2)}) copy-start(bf16[1536,256]{1,0:T(8,128)(2,1)S(1)} %slice_dynamic-update-slice_fusion.refs_0_) | copy-start | bytes 2359300
  88.6 21.6 %copy-start.11 = (bf16[768,512]{1,0:T(8,128)(2,1)}, bf16[768,512]{1,0:T(8,128)(2,1)S(1)}, u32[]{:S(2)}) copy-start(bf16[768,512]{1,0:T(8,128)(2,1)S(1)} %collective-permute-done.4.refs_1_) | copy-start | bytes 2359300
  88.6 31.2 %collective-permute-start.5 = (bf16[768,512]{1,0:T(8,128)(2,1)S(1)}, bf16[768,512]{1,0:T(8,128)(2,1)S(1)}, u32[]{:S(2)}, u32[]{:S(2)}) collective-permute-start(bf16[768,512]{1,0:T(8,128)(2,1)S(1)} %collective-permute-done.4.refs_1_), channel_id=1, source_target_pairs={{0,16},{8,120},{16,32},{24,8},{32,48},{40,24},{48,64},{56,40},{64,... | collective-permute-start | bytes 2359304 | tf_op jit(solution)/shard_map/ppermute | solution.py:275
  97.0 22.9 %collective-permute-start.9 = (bf16[768,512]{1,0:T(8,128)(2,1)}, bf16[768,512]{1,0:T(8,128)(2,1)S(1)}, u32[]{:S(2)}, u32[]{:S(2)}) collective-permute-start(bf16[768,512]{1,0:T(8,128)(2,1)} %collective-permute-done.8.refs_2_), channel_id=1, source_target_pairs={{0,16},{8,120},{16,32},{24,8},{32,48},{40,24},{48,64},{56,40},{64,... | collective-permute-start | bytes 2359304 | tf_op jit(solution)/shard_map/ppermute | solution.py:275
  119.7 1.0 copy-start.7
  119.8 18.1 %collective-permute-start.6 = (bf16[384,512]{1,0:T(8,128)(2,1)S(1)}, bf16[384,512]{1,0:T(8,128)(2,1)S(1)}, u32[]{:S(2)}, u32[]{:S(2)}) collective-permute-start(bf16[384,512]{1,0:T(8,128)(2,1)S(1)} %slice.63), channel_id=1, source_target_pairs={{0,16},{8,120},{16,32},{24,8},{32,48},{40,24},{48,64},{56,40},{64,... | collective-permute-start | bytes 1179656 | tf_op jit(solution)/shard_map/ppermute | solution.py:275
  119.9 10.4 %copy-start.1 = (bf16[768,512]{1,0:T(8,128)(2,1)}, bf16[768,512]{1,0:T(8,128)(2,1)S(1)}, u32[]{:S(2)}) copy-start(bf16[768,512]{1,0:T(8,128)(2,1)S(1)} %collective-permute-done.9.refs_1_) | copy-start | bytes 2359300
  119.9 18.0 %collective-permute-start.10 = (bf16[384,512]{1,0:T(8,128)(2,1)S(1)}, bf16[384,512]{1,0:T(8,128)(2,1)S(1)}, u32[]{:S(2)}, u32[]{:S(2)}) collective-permute-start(bf16[384,512]{1,0:T(8,128)(2,1)S(1)} %slice.66), channel_id=1, source_target_pairs={{0,16},{8,120},{16,32},{24,8},{32,48},{40,24},{48,64},{56,40},{64,... | collective-permute-start | bytes 1179656 | tf_op jit(solution)/shard_map/ppermute | solution.py:275
  137.9 0.7 copy-start.2
  138.6 0.7 copy-start.3
  144.2 5.5 %collective-permute-start.11 = (bf16[768,256]{1,0:T(8,128)(2,1)}, bf16[768,256]{1,0:T(8,128)(2,1)S(1)}, u32[]{:S(2)}, u32[]{:S(2)}) collective-permute-start(bf16[768,256]{1,0:T(8,128)(2,1)} %get-tuple-element.15), channel_id=1, source_target_pairs={{0,8},{8,0},{1,9},{9,1},{2,10},{10,2},{3,11},{11,3},{4,12},{12,4},... | collective-permute-start | bytes 1179656 | tf_op jit(solution)/shard_map/ppermute | solution.py:277
  144.6 5.1 %collective-permute-start.12 = (f32[768,128]{1,0:T(8,128)}, f32[768,128]{1,0:T(8,128)S(1)}, u32[]{:S(2)}, u32[]{:S(2)}) collective-permute-start(f32[768,128]{1,0:T(8,128)} %get-tuple-element.16), channel_id=1, source_target_pairs={{0,8},{8,0},{1,9},{9,1},{2,10},{10,2},{3,11},{11,3},{4,12},{12,4},... | collective-permute-start | bytes 1179656 | tf_op jit(solution)/shard_map/ppermute | solution.py:277
  149.7 0.8 copy-start.5
  149.7 0.9 copy-start.6
  153.9 15.2 %collective-permute-start.13 = (bf16[384,256]{1,0:T(8,128)(2,1)}, bf16[384,256]{1,0:T(8,128)(2,1)S(1)}, u32[]{:S(2)}, u32[]{:S(2)}) collective-permute-start(bf16[384,256]{1,0:T(8,128)(2,1)} %get-tuple-element.18), channel_id=1, source_target_pairs={{0,128},{128,0},{1,129},{129,1},{2,130},{130,2},{3,131},{131,3},{4... | collective-permute-start | bytes 589832 | tf_op jit(solution)/shard_map/ppermute | solution.py:276
  169.0 0.7 copy-start.8
